TPU v7x, 256 devices: a whole 4x4x8 slice. The times are simulated.
256 devices in a mesh: row: 8 (over x, core), col: 32 (over z, y).
Axes of the slice: x: 4, y: 4, z: 8, core: 2. Of those that a mesh axis runs over, the one named last changes fastest.
Arguments:
- source_points: bfloat16 [16384, 256], P(('row', 'col')), may hold values from -96 to 96
- target_points: bfloat16 [65536, 256], P(('col', 'row')), may hold values from -6 to 6
- source_weight: float32 [16384], P('row'), may hold values from 0.25 to 4
- target_weight: float32 [65536], P('col'), may hold values from 0.25 to 4
- target_potential: float32 [65536], P('col'), may hold values from -8 to 104
Outputs:
- source_potential: float32 [16384], P('row')
- target_updated: float32 [65536], P('col')
All inputs are finite; a program needn't handle non-finite values.
Results may differ from a plain program's by a relative error of at most 0.0003.
Values may be sent and summed in bfloat16 or wider, within the bound.
No kernel may reach another device: no remote copies, remote signals or barrier semaphores. Data moves between devices by JAX's collectives and lax.ppermute only.
A program may use at most 64 MiB of HBM per device.

v0:
```python
import math

import jax
import jax.numpy as jnp
from jax import lax
from jax.sharding import PartitionSpec as P

EPSILON = 0.25


def update_rows(maxima, totals, logits):
    highest = jnp.maximum(maxima, jnp.max(logits, axis=1))
    totals = jnp.sum(jnp.exp(logits - highest[:, None]), axis=1)
    return (highest, totals)


def update_cols(maxima, totals, logits):
    highest = jnp.maximum(maxima, jnp.max(logits, axis=0))
    totals = totals * jnp.exp(maxima - highest) + jnp.sum(
        jnp.exp(logits - highest[None, :]), axis=0
    )
    return (highest, totals)


def per_device(source_points, target_points, source_weight, target_weight, target_potential):
    width = source_points.shape[1]
    inverse_temp = 1.0 / (EPSILON * math.sqrt(width))
    sources = lax.all_gather(source_points, "col", axis=0, tiled=True)
    source_count = sources.shape[0]
    target_count = target_potential.shape[0]
    floor_rows = jnp.full((source_count,), -1e30, jnp.float32)
    zero_rows = jnp.zeros((source_count,), jnp.float32)
    empty_targets = jnp.zeros((target_count, width), jnp.bfloat16)
    start_state = (floor_rows, zero_rows, empty_targets)
    shard_rows = lax.all_gather(target_points, "row", axis=0, tiled=True)
    piece_similar = jnp.einsum("id,jd->ij", sources, shard_rows, preferred_element_type=jnp.float32)
    fold_logits = target_potential[None, :] + inverse_temp * piece_similar
    maxima, totals = update_rows(start_state[0], start_state[1], fold_logits)
    row_max = maxima
    row_total = totals
    global_max = lax.pmax(row_max, "col")
    row_total = lax.psum(row_total * jnp.exp(row_max - global_max), "col")
    row_max = global_max
    target_all = target_count * lax.axis_size("col")
    source_potential = jnp.log(source_weight) - (
        row_max + jnp.log(row_total) - jnp.float32(math.log(target_all))
    )
    block_rows = min(512, source_count)
    col_max = jnp.full((target_count,), -1e30, jnp.float32)
    col_total = jnp.zeros((target_count,), jnp.float32)
    for first_row in range(0, source_count, block_rows):
        similar = jnp.einsum(
            "id,jd->ij",
            sources[first_row : first_row + block_rows],
            shard_rows,
            preferred_element_type=jnp.float32,
        )
        logits = source_potential[first_row : first_row + block_rows, None] + inverse_temp * similar
        col_max, col_total = update_cols(col_max, col_total, logits)
    global_col = lax.pmax(col_max, "row")
    col_total = lax.psum(col_total * jnp.exp(col_max - global_col), "row")
    col_max = global_col
    source_all = source_count * lax.axis_size("row")
    target_updated = jnp.log(target_weight) - (
        col_max + jnp.log(col_total) - jnp.float32(math.log(source_all))
    )
    return (source_potential, target_updated)


def solution(mesh):
    return jax.shard_map(
        per_device,
        mesh=mesh,
        in_specs=(P(("row", "col"), None), P(("col", "row"), None), P("row"), P("col"), P("col")),
        out_specs=(P("row"), P("col")),
        check_vma=False,
    )
```

profile of v0, /device:TPU:1, one launch (start us, length us, event | category | flops | bytes accessed | tf_op | source)
XLA Modules:
  0.0 331.8 jit_solution(11539796141535999254)
XLA Ops:
  7.2 0.0 all-gather.5.cloned.1.call-start
  7.2 0.7 all-gather.5.cloned.1.call-update
  7.9 0.0 all-gather.3.cloned.1.call-start
  7.9 0.7 all-gather.3.cloned.1.call-update
  8.6 0.0 copy-start.4
  8.7 31.3 %all-gather.5.cloned.1.call-done = bf16[2048,256]{1,0:T(8,128)(2,1)} async-done(((bf16[256,256]{1,0:T(8,128)(2,1)}), bf16[2048,256]{1,0:T(8,128)(2,1)}) %all-gather.5.cloned.1.call-update) | async-done | bytes 1048592 | tf_op jit(solution)/shard_map/all_gather | solution.py:35
  40.0 73.9 %all-gather.3.cloned.1.call-done = bf16[2048,256]{1,0:T(8,128)(2,1)} async-done(((bf16[64,256]{1,0:T(8,128)(2,1)}), bf16[2048,256]{1,0:T(8,128)(2,1)}) %all-gather.3.cloned.1.call-update) | async-done | bytes 1048592 | tf_op jit(solution)/shard_map/all_gather | solution.py:28
  113.9 9.6 %fusion = (f32[2048]{0:T(1024)S(1)}, f32[2048,2048]{0,1:T(8,128)}) fusion(f32[2048]{0:T(1024)} %param.9, bf16[2048,256]{1,0:T(8,128)(2,1)} %all-gather.3.cloned.1.call-done, bf16[2048,256]{1,0:T(8,128)(2,1)} %all-gather.5.cloned.1.call-done), kind=kOutput, calls=%fused_computation.2 | convolution fusion | flops 2160064512 | bytes 18890752 | tf_op jit(solution)/shard_map/id,jd->ij/dot_general | solution.py:36
  123.6 59.0 %pmax.14 = f32[2048]{0:T(1024)S(1)} all-reduce(f32[2048]{0:T(1024)S(1)} %broadcast_maximum_fusion.1), channel_id=1, replica_groups=mesh['row'=8,'col'=32] {'col'}, use_global_device_ids=true, to_apply=%region_1.0 | all-reduce | flops 2048 | bytes 16384 | tf_op jit(solution)/shard_map/pmax | solution.py:41
  182.6 0.0 copy-done.4
  182.6 0.0 copy-start.6
  182.6 0.0 copy-start
  182.6 0.0 copy-start.3
  182.6 8.1 %exponential_reduce_fusion = f32[2048]{0:T(1024)S(1)} fusion(f32[2048,2048]{0,1:T(8,128)} %get-tuple-element.11, f32[2048]{0:T(1024)S(1)} %broadcast_maximum_fusion.1, f32[2048]{0:T(1024)S(1)} %copy-done.4), kind=kLoop, calls=%fused_computation | loop fusion | flops 16775168 | bytes 16801792 | tf_op jit(solution)/shard_map/reduce_sum | solution.py:13
  190.8 56.9 %psum.14 = f32[2048]{0:T(1024)S(1)} all-reduce(f32[2048]{0:T(1024)S(1)} %exponential_multiply_fusion.1), channel_id=1, replica_groups=mesh['row'=8,'col'=32] {'col'}, use_global_device_ids=true, to_apply=%region_3.0 | all-reduce | flops 2048 | bytes 16384 | tf_op jit(solution)/shard_map/psum | solution.py:42
  247.7 0.0 copy-done.6
  247.7 0.0 copy-start.5
  247.8 0.0 copy-done
  247.8 0.0 copy-done.3
  247.8 2.7 fusion.1
  250.5 2.7 fusion.4
  253.2 2.7 fusion.3
  255.9 2.7 fusion.2
  258.6 45.1 %pmax.15 = f32[2048]{0:T(1024)S(1)} all-reduce(f32[2048]{0:T(1024)S(1)} %get-tuple-element.2), channel_id=1, replica_groups=mesh['row'=8,'col'=32] {'row'}, use_global_device_ids=true, to_apply=%region_8.0 | all-reduce | flops 2048 | bytes 16384 | tf_op jit(solution)/shard_map/pmax | solution.py:60
  303.7 0.0 copy-start.1
  303.7 0.0 copy-start.2
  303.7 4.6 %exponential_reduce_fusion.1 = (f32[2048]{0:T(1024)S(1)}, f32[2048]{0:T(1024)S(1)}) fusion(f32[512,2048]{1,0:T(8,128)} %get-tuple-element.13, f32[2048]{0:T(1024)S(1)} %get-tuple-element.2, f32[512]{0:T(512)S(1)} %get-tuple-element.7, f32[2048]{0:T(1024)S(1)} %get-tuple-element.3, f32[512,2048]{1,0:T(8,128)} %get-tuple-element.15, f32[512]{0:T(512)S(1)} %get-tuple-element.8), kind=kLoop, calls=%fused_computation.3 | loop fusion | flops 8384512 | bytes 8425472 | tf_op jit(solution)/shard_map/reduce_sum | solution.py:19
  308.3 0.0 copy-done.1
  308.4 1.3 copy-done.2
  309.6 2.0 exponential_reduce_fusion.3
  311.7 12.7 %psum.15 = f32[2048]{0:T(1024)S(1)} all-reduce(f32[2048]{0:T(1024)S(1)} %exponential_multiply_fusion), channel_id=1, replica_groups=mesh['row'=8,'col'=32] {'row'}, use_global_device_ids=true, to_apply=%region_13.0 | all-reduce | flops 2048 | bytes 16384 | tf_op jit(solution)/shard_map/psum | solution.py:61
  324.4 0.6 add_subtract_fusion
  (9 shorter events, 0.1 us)
Async XLA Ops:
  7.2 32.8 %all-gather.5.cloned.1.call-start = ((), (), s32[]{:S(2)}) async-start(), calls=%async_computation.1 | async-start | bytes 1179648 | tf_op jit(solution)/shard_map/all_gather | solution.py:35
  7.9 106.0 %all-gather.3.cloned.1.call-start = ((), (), s32[]{:S(2)}) async-start(), calls=%async_computation | async-start | bytes 1081344 | tf_op jit(solution)/shard_map/all_gather | solution.py:28
  8.6 173.9 %copy-start.4 = (f32[2048]{0:T(1024)S(1)}, f32[2048]{0:T(1024)}, u32[]{:S(2)}) copy-start(f32[2048]{0:T(1024)} %param.9) | copy-start | bytes 24580
  182.6 65.1 %copy-start.6 = (f32[2048]{0:T(1024)S(1)}, f32[2048]{0:T(1024)}, u32[]{:S(2)}) copy-start(f32[2048]{0:T(1024)} %param.7) | copy-start | bytes 24580
  182.6 65.2 %copy-start = (bf16[2048,256]{1,0:T(8,128)(2,1)S(1)}, bf16[2048,256]{1,0:T(8,128)(2,1)}, u32[]{:S(2)}) copy-start(bf16[2048,256]{1,0:T(8,128)(2,1)} %all-gather.5.cloned.1.call-done) | copy-start | bytes 3145732
  182.6 65.2 %copy-start.3 = (bf16[2048,256]{1,0:T(8,128)(2,1)S(1)}, bf16[2048,256]{1,0:T(8,128)(2,1)}, u32[]{:S(2)}) copy-start(bf16[2048,256]{1,0:T(8,128)(2,1)} %all-gather.3.cloned.1.call-done) | copy-start | bytes 3145732
  247.7 5.5 %copy-start.5 = (f32[2048]{0:T(1024)}, f32[2048]{0:T(1024)S(1)}, u32[]{:S(2)}) copy-start(f32[2048]{0:T(1024)S(1)} %add_subtract_fusion.1) | copy-start | bytes 24580
  303.7 4.7 %copy-start.1 = (f32[512,2048]{1,0:T(8,128)S(1)}, f32[512,2048]{1,0:T(8,128)}, u32[]{:S(2)}) copy-start(f32[512,2048]{1,0:T(8,128)} %get-tuple-element.19) | copy-start | bytes 12582916
  303.7 5.9 %copy-start.2 = (f32[512,2048]{1,0:T(8,128)S(1)}, f32[512,2048]{1,0:T(8,128)}, u32[]{:S(2)}) copy-start(f32[512,2048]{1,0:T(8,128)} %get-tuple-element.17) | copy-start | bytes 12582916
  309.6 14.7 %copy-start.7 = (f32[2048]{0:T(1024)S(1)}, f32[2048]{0:T(1024)}, u32[]{:S(2)}) copy-start(f32[2048]{0:T(1024)} %param.8) | copy-start | bytes 24580
Sparse Core Ops, SparseCore 0:
  9.9 30.0 all-gather.4
  42.6 71.2 all-gather.2
where the time goes:
time: 332 us
  blocking collectives  174 us (52%)
  waiting for transfers between devices  107 us (32%)
  matrix products  20.5 us (6%)
  other arithmetic  15.4 us (5%)
  between operations  14.2 us (4%)
    all_gather x1, waiting for transfers between devices, per_device(): sources = lax.all_gather(source_points, 'col', axis=0, tiled=True)  73.9 us
    pmax x1, blocking collectives, per_device(): global_max = lax.pmax(row_max, 'col')  59 us
    psum x1, blocking collectives, per_device(): row_total = lax.psum(row_total * jnp.exp(row_max - global_max), 'col')  56.9 us
    pmax x1, blocking collectives, per_device(): global_col = lax.pmax(col_max, 'row')  45.1 us
    all_gather x1, waiting for transfers between devices, per_device(): shard_rows = lax.all_gather(target_points, 'row', axis=0, tiled=True)  31.3 us
    psum x1, blocking collectives, per_device(): col_total = lax.psum(col_total * jnp.exp(col_max - global_col), 'row')  12.7 us
    dot_general x4, matrix products, per_device(): jnp.einsum('id,jd->ij', sources[first_row:first_row + block_rows], shard_...  10.8 us
    dot_general x1, matrix products, per_device(): jnp.einsum('id,jd->ij', sources, shard_rows, preferred_element_type=jnp.f...  9.65 us
  transfers between devices with their start and end apart: 2, of which 2 were waited for; matrix products, arithmetic and copies ran while one was open for 0% of the time, Pallas kernels for 0%

commit v1 on v0

v1 whole, which is shorter than its diff:
```python
import functools
import math

import jax
import jax.numpy as jnp
from jax import lax
from jax.experimental import pallas as pl
from jax.experimental.pallas import tpu as pltpu
from jax.sharding import Mesh
from jax.sharding import PartitionSpec as P

EPSILON = 0.25
LANES = 128
STRIP = 256
NX, NC, NZ, NY = 4, 2, 8, 4
SHIFTS = (0, 1, 3, 2)
VMEM = pl.BlockSpec(memory_space=pltpu.VMEM)
PARAMS = pltpu.CompilerParams(vmem_limit_bytes=40 * 1024 * 1024)


def contract(a, b):
    return lax.dot_general(a, b, (((1,), (1,)), ((), ())), preferred_element_type=jnp.float32)


def spread(row):
    return jnp.broadcast_to(row, (LANES, LANES)).T


def lse_of(buf, bias, rate):
    rows = buf.shape[0]
    step = 64
    out = []
    for half in range(STRIP // LANES):
        lanes = slice(half * LANES, (half + 1) * LANES)
        top = None
        for r in range(0, rows, step):
            value = buf[r : r + step, lanes] + bias[r : r + step, :]
            buf[r : r + step, lanes] = value
            top = value if top is None else jnp.maximum(top, value)
        top = jnp.max(top, axis=0, keepdims=True)
        total = None
        for r in range(0, rows, step):
            value = jnp.exp2((buf[r : r + step, lanes] - top) * rate)
            total = value if total is None else total + value
        total = jnp.sum(total, axis=0, keepdims=True)
        out.append(top + jnp.log2(total) / rate)
    return out


def all_strips(count, fill, finish, buf0, buf1):
    fill(0, buf0)

    def pair(p, _):
        fill(2 * p + 1, buf1)
        finish(2 * p, buf0)
        fill(jnp.minimum(2 * p + 2, count - 1), buf0)
        finish(2 * p + 1, buf1)
        return 0

    lax.fori_loop(0, count // 2, pair, 0)


def bias_kernel(tp_ref, bias_ref):
    x, c = lax.axis_index("x"), lax.axis_index("c")
    row = 0
    for other in range(NC):
        for k in SHIFTS:
            block = lax.rem(x - k + NX, NX) * NC + lax.rem(c + other, NC)
            for half in range(2):
                values = tp_ref[pl.ds(block * 2 + half, 1), :] * (1.0 / bias_kernel.scale)
                bias_ref[row * LANES : (row + 1) * LANES, :] = spread(values)
                row += 1


def row_kernel(rate, last, *refs):
    if last:
        s_ref, ta_ref, tb_ref, bias_ref, l0, l1, l2, out_ref, buf0, buf1, rows = refs
    else:
        s_ref, ta_ref, tb_ref, bias_ref, out_ref, buf0, buf1 = refs
    half = ta_ref.shape[0]
    got = []
    for n, buf in enumerate((buf0, buf1)):
        strip = s_ref[n * STRIP : (n + 1) * STRIP, :]
        buf[:half, :] = contract(ta_ref[...], strip)
        buf[half:, :] = contract(tb_ref[...], strip)
    for buf in (buf0, buf1):
        got += lse_of(buf, bias_ref, rate)
    mine = jnp.concatenate(got, axis=0)
    if not last:
        out_ref[...] = mine
        return
    y = lax.axis_index("y")
    for k, values in zip(SHIFTS, (l0[...], l1[...], l2[...], mine)):
        at = lax.rem(y - k + NY, NY) * 4
        for i in range(4):
            rows[pl.ds(at + i, 1), :] = values[i : i + 1, :]
    out_ref[...] = jnp.broadcast_to(rows[...][None], out_ref.shape)


def col_kernel(rate, scale, offset, got_ref, sw_ref, s0, s1, s2, s3, ta_ref, tb_ref, out_ref, sp_ref, buf0, buf1, bias, spu, cols):
    parts = got_ref[...]
    top = jnp.max(parts, axis=0)
    total = jnp.sum(jnp.exp2((parts - top[None]) * rate), axis=0)
    lse = top + jnp.log2(total) / rate
    sp = jnp.log(sw_ref[...]) - (lse * scale - offset)
    sp_ref[...] = sp
    spu[...] = sp * (1.0 / scale)
    x, c, y = lax.axis_index("x"), lax.axis_index("c"), lax.axis_index("y")
    row = 0
    for k in SHIFTS:
        at = lax.rem(y - k + NY, NY) * 4
        for i in range(4):
            bias[row * LANES : (row + 1) * LANES, :] = spread(spu[pl.ds(at + i, 1), :])
            row += 1
    chunk = s0.shape[0]
    for other, t_ref in enumerate((ta_ref, tb_ref)):
        core = lax.rem(c + other, NC)

        def fill(n, buf, t_ref=t_ref):
            strip = t_ref[pl.ds(pl.multiple_of(n * STRIP, STRIP), STRIP), :]
            for k, s_ref in enumerate((s0, s1, s2, s3)):
                buf[k * chunk : (k + 1) * chunk, :] = contract(s_ref[...], strip)

        def finish(n, buf, core=core):
            lo, hi = lse_of(buf, bias, rate)
            k = jnp.where(n == 2, 3, jnp.where(n == 3, 2, n))
            block = lax.rem(x - k + NX, NX) * NC + core
            cols[pl.ds(block * 2, 1), :] = lo
            cols[pl.ds(block * 2 + 1, 1), :] = hi

        all_strips(NX, fill, finish, buf0, buf1)
    out_ref[...] = jnp.broadcast_to(cols[...][None], out_ref.shape)


def last_kernel(rate, scale, offset, got_ref, tw_ref, out_ref):
    parts = got_ref[...]
    top = jnp.max(parts, axis=0)
    total = jnp.sum(jnp.exp2((parts - top[None]) * rate), axis=0)
    lse = top + jnp.log2(total) / rate
    out_ref[...] = jnp.log(tw_ref[...]) - (lse * scale - offset)


def cost(pairs, width):
    return pl.CostEstimate(flops=2 * pairs * width, bytes_accessed=8 * 1024 * 1024, transcendentals=pairs)


def per_device(source_points, target_points, source_weight, target_weight, target_potential):
    width = source_points.shape[1]
    scale = 1.0 / (EPSILON * math.sqrt(width))
    rate = scale * math.log2(math.e)
    n_rows, n_cols = source_weight.shape[0], target_weight.shape[0]
    f32 = jnp.float32
    sub = n_rows // LANES

    around = lambda n, k: [(i, (i + k) % n) for i in range(n)]
    pieces = [target_points] + [lax.ppermute(target_points, "x", around(NX, k)) for k in SHIFTS[1:]]
    near = jnp.concatenate(pieces, axis=0)
    far = lax.ppermute(near, "c", around(NC, 1))
    own = lax.all_to_all(jnp.broadcast_to(source_points[None], (NZ,) + source_points.shape), "z", 0, 0)
    own = own.reshape(-1, width)
    chunks = [own] + [lax.ppermute(own, "y", around(NY, k)) for k in SHIFTS[1:]]
    chunk = own.shape[0]

    bias_kernel.scale = scale
    bias = pl.pallas_call(
        bias_kernel,
        out_shape=jax.ShapeDtypeStruct((n_cols, LANES), f32),
        in_specs=[VMEM],
        out_specs=VMEM,
        compiler_params=PARAMS,
    )(target_potential.reshape(-1, LANES))

    bufs = [pltpu.VMEM((n_cols, STRIP), f32)] * 2
    lses = []
    for n in range(3):
        lses.append(
            pl.pallas_call(
                functools.partial(row_kernel, rate, False),
                out_shape=jax.ShapeDtypeStruct((chunk // LANES, LANES), f32),
                in_specs=[VMEM] * 4,
                out_specs=VMEM,
                scratch_shapes=bufs,
                compiler_params=PARAMS,
                cost_estimate=cost(chunk * n_cols, width),
            )(chunks[n], near, far, bias)
        )
    sent = pl.pallas_call(
        functools.partial(row_kernel, rate, True),
        out_shape=jax.ShapeDtypeStruct((NZ * NY, sub, LANES), f32),
        in_specs=[VMEM] * 7,
        out_specs=VMEM,
        scratch_shapes=bufs + [pltpu.VMEM((sub, LANES), f32)],
        compiler_params=PARAMS,
        cost_estimate=cost(chunk * n_cols, width),
    )(chunks[3], near, far, bias, *lses)
    got = lax.all_to_all(sent, ("z", "y"), 0, 0)

    small = n_rows // (NZ * NY)
    weight = source_weight.reshape(NZ, NY, small).transpose(1, 0, 2).reshape(sub, LANES)
    sent, potential = pl.pallas_call(
        functools.partial(col_kernel, rate, scale, math.log(n_cols * NZ * NY)),
        out_shape=[
            jax.ShapeDtypeStruct((NX * NC, n_cols // LANES, LANES), f32),
            jax.ShapeDtypeStruct((sub, LANES), f32),
        ],
        in_specs=[VMEM] * 8,
        out_specs=[VMEM] * 2,
        scratch_shapes=bufs
        + [pltpu.VMEM((n_rows, LANES), f32), pltpu.VMEM((sub, LANES), f32), pltpu.VMEM((n_cols // LANES, LANES), f32)],
        compiler_params=PARAMS,
        cost_estimate=cost(n_rows * n_cols, width),
    )(got, weight, *chunks, near, far)
    got = lax.all_to_all(sent, ("x", "c"), 0, 0)
    updated = pl.pallas_call(
        functools.partial(last_kernel, rate, scale, math.log(n_rows * NX * NC)),
        out_shape=jax.ShapeDtypeStruct((n_cols // LANES, LANES), f32),
        in_specs=[VMEM] * 2,
        out_specs=VMEM,
        compiler_params=PARAMS,
    )(got, target_weight.reshape(-1, LANES))
    potential = potential.reshape(NY, NZ, small).transpose(1, 0, 2).reshape(-1)
    return potential, updated.reshape(-1)


def solution(mesh):
    grid = Mesh(mesh.devices.reshape(NX, NC, NZ, NY), ("x", "c", "z", "y"))
    return jax.shard_map(
        per_device,
        mesh=grid,
        in_specs=(P(("x", "c", "z", "y"), None), P(("z", "y", "x", "c"), None), P(("x", "c")), P(("z", "y")), P(("z", "y"))),
        out_specs=(P(("x", "c")), P(("z", "y"))),
        check_vma=False,
    )
```

time: 332 us -> 79.8 us (0.24)
  blocking collectives: 174 us -> 0 us
  waiting for transfers between devices: 107 us -> 26.7 us
  starting transfers between devices: 0.08 us -> 35 us
  matrix products: 20.5 us -> 0 us
  other arithmetic: 15.4 us -> 0 us
  Pallas kernels: 0 us -> 14.4 us
  between operations: 14.2 us -> 0.77 us
    all_gather x2 -> x0, waiting for transfers between devices: 105 us -> none  [the longest x1 73.9 us: per_device(): sources = lax.all_gather(source_points, 'col', axis=0, tiled=True)]
    pmax x2 -> x0, blocking collectives: 104 us -> none  [the longest x1 59 us: per_device(): global_max = lax.pmax(row_max, 'col')]
    psum x2 -> x0, blocking collectives: 69.6 us -> none  [the longest x1 56.9 us: per_device(): row_total = lax.psum(row_total * jnp.exp(row_max - global_max), 'col')]
    all_to_all x0 -> x3, starting transfers between devices: none -> 23.6 us  [the longest x1 9.63 us: per_device(): got = lax.all_to_all(sent, ('x', 'c'), 0, 0)]
    all_to_all x0 -> x3, waiting for transfers between devices: none -> 21.6 us  [the longest x1 10.1 us: per_device(): got = lax.all_to_all(sent, ('z', 'y'), 0, 0)]
    dot_general x5 -> x0, matrix products: 20.5 us -> none  [the longest x4 10.8 us: per_device(): jnp.einsum('id,jd->ij', sources[first_row:first_row + block_rows], shard_...]
    reduce_sum x3 -> x0, other arithmetic: 14.7 us -> none  [the longest x1 8.13 us: update_rows(): totals = jnp.sum(jnp.exp(logits - highest[:, None]), axis=1)]
    pallas_call x0 -> x7, Pallas kernels: none -> 14.4 us  [the longest x1 7.23 us: per_device(): pl.pallas_call(functools.partial(col_kernel, rate, scale, math.log(n_cols...]
  transfers between devices with their start and end apart: 2 -> 10, of which waited for: 2 -> 4; matrix products, arithmetic and copies ran while one was open for 0% -> 3% of each run, Pallas kernels for 0% -> 6%
where the time goes in v1:
time: 79.8 us; the launch traced here: 79.4 us
  starting transfers between devices  35 us (44%)
  waiting for transfers between devices  26.7 us (33%)
  Pallas kernels  14.4 us (18%)
  local copies, waits for them, and re-layouts  2.44 us (3%)
    all_to_all x1, waiting for transfers between devices, per_device(): got = lax.all_to_all(sent, ('z', 'y'), 0, 0)  10.1 us
    all_to_all x1, starting transfers between devices, per_device(): got = lax.all_to_all(sent, ('x', 'c'), 0, 0)  9.63 us
    all_to_all x1, starting transfers between devices, per_device(): lax.all_to_all(jnp.broadcast_to(source_points[None], (NZ,) + source_point...  8.32 us
    all_to_all x1, waiting for transfers between devices, per_device(): lax.all_to_all(jnp.broadcast_to(source_points[None], (NZ,) + source_point...  7.48 us
    pallas_call x1, Pallas kernels, per_device(): pl.pallas_call(functools.partial(col_kernel, rate, scale, math.log(n_cols...  7.23 us
    all_to_all x1, starting transfers between devices, per_device(): got = lax.all_to_all(sent, ('z', 'y'), 0, 0)  5.66 us
    ppermute x3, starting transfers between devices, per_device(): lax.ppermute(target_points, 'x', around(NX, k))  5.12 us
    ppermute x3, waiting for transfers between devices, per_device(): chunks = [own] + [lax.ppermute(own, 'y', around(NY, k)) for k in SHIFTS[1:]]  5.09 us
  transfers between devices with their start and end apart: 10, of which 4 were waited for; matrix products, arithmetic and copies ran while one was open for 3% of the time, Pallas kernels for 6%

profile of v1, /device:TPU:1, one launch (start us, length us, event | category | flops | bytes accessed | tf_op | source)
XLA Modules:
  0.0 79.4 jit_solution(2692971852069990118)
XLA Ops:
  0.6 2.1 %collective-permute-start.1 = (bf16[256,256]{1,0:T(8,128)(2,1)}, bf16[256,256]{1,0:T(8,128)(2,1)S(1)}, u32[]{:S(2)}, u32[]{:S(2)}) collective-permute-start(bf16[256,256]{1,0:T(8,128)(2,1)} %param.6), channel_id=1, source_target_pairs={{0,64},{64,128},{128,192},{192,0},{1,65},{65,129},{129,193},{193,1... | collective-permute-start | bytes 393224 | tf_op jit(solution)/shard_map/ppermute | solution.py:156
  2.7 1.4 %collective-permute-start.2 = (bf16[256,256]{1,0:T(8,128)(2,1)}, bf16[256,256]{1,0:T(8,128)(2,1)S(1)}, u32[]{:S(2)}, u32[]{:S(2)}) collective-permute-start(bf16[256,256]{1,0:T(8,128)(2,1)} %param.6), channel_id=1, source_target_pairs={{0,192},{64,0},{128,64},{192,128},{1,193},{65,1},{129,65},{193,129... | collective-permute-start | bytes 393224 | tf_op jit(solution)/shard_map/ppermute | solution.py:156
  4.1 1.6 %collective-permute-start.3 = (bf16[256,256]{1,0:T(8,128)(2,1)}, bf16[256,256]{1,0:T(8,128)(2,1)S(1)}, u32[]{:S(2)}, u32[]{:S(2)}) collective-permute-start(bf16[256,256]{1,0:T(8,128)(2,1)} %param.6), channel_id=1, source_target_pairs={{0,128},{64,192},{128,0},{192,64},{1,129},{65,193},{129,1},{193,65... | collective-permute-start | bytes 393224 | tf_op jit(solution)/shard_map/ppermute | solution.py:156
  5.7 1.5 %broadcast_in_dim.2 = bf16[8,64,256]{2,1,0:T(8,128)(2,1)} broadcast(bf16[64,256]{1,0:T(8,128)(2,1)} %param.5), dimensions={1,2} | broadcast | bytes 294912 | tf_op jit(solution)/shard_map/broadcast_in_dim | solution.py:159
  7.2 8.3 %all-to-all-start = ((bf16[8,64,256]{2,1,0:T(8,128)(2,1)}), bf16[8,64,256]{2,1,0:T(8,128)(2,1)S(1)}, u32[]{:S(2)}, u32[]{:S(2)}) async-start(bf16[8,64,256]{2,1,0:T(8,128)(2,1)} %broadcast_in_dim.2), calls=%async_computation | async-start | bytes 524288 | tf_op jit(solution)/shard_map/all_to_all | solution.py:159
  15.6 0.0 collective-permute-done.1
  15.6 0.0 collective-permute-done.2
  15.6 0.0 collective-permute-done.3
  15.6 0.0 copy-start
  15.7 1.9 %collective-permute-start.4 = (bf16[1024,256]{1,0:T(8,128)(2,1)S(1)}, bf16[1024,256]{1,0:T(8,128)(2,1)S(1)}, u32[]{:S(2)}, u32[]{:S(2)}) collective-permute-start(bf16[1024,256]{1,0:T(8,128)(2,1)S(1)} %constant_dynamic-update-slice_fusion.refs_1_.ta_ref), channel_id=1, source_target_pairs={{0,32},{32,0},{1,33},{33,1},{2,34},{34,2},{3,35},{35,3},{4,36},{36... | collective-permute-start | bytes 1572872 | tf_op jit(solution)/shard_map/ppermute | solution.py:158
  17.5 7.5 %all-to-all-done = bf16[8,64,256]{2,1,0:T(8,128)(2,1)S(1)} async-done(((bf16[8,64,256]{2,1,0:T(8,128)(2,1)}), bf16[8,64,256]{2,1,0:T(8,128)(2,1)S(1)}, u32[]{:S(2)}, u32[]{:S(2)}) %all-to-all-start) | async-done | bytes 262176 | tf_op jit(solution)/shard_map/all_to_all | solution.py:159
  25.0 2.7 %collective-permute-start.6 = (bf16[512,256]{1,0:T(8,128)(2,1)S(1)}, bf16[512,256]{1,0:T(8,128)(2,1)S(1)}, u32[]{:S(2)}, u32[]{:S(2)}) collective-permute-start(bf16[512,256]{1,0:T(8,128)(2,1)S(1)} %bitcast.8), channel_id=1, source_target_pairs={{0,3},{1,0},{2,1},{3,2},{4,7},{5,4},{6,5},{7,6},{8,11},{9,8},{10,9... | collective-permute-start | bytes 786440 | tf_op jit(solution)/shard_map/ppermute | solution.py:161
  27.8 0.0 collective-permute-start.5
  27.8 1.6 %collective-permute-start = (bf16[512,256]{1,0:T(8,128)(2,1)S(1)}, bf16[512,256]{1,0:T(8,128)(2,1)S(1)}, u32[]{:S(2)}, u32[]{:S(2)}) collective-permute-start(bf16[512,256]{1,0:T(8,128)(2,1)S(1)} %bitcast.10), channel_id=1, source_target_pairs={{0,2},{1,3},{2,0},{3,1},{4,6},{5,7},{6,4},{7,5},{8,10},{9,11},{10,... | collective-permute-start | bytes 786440 | tf_op jit(solution)/shard_map/ppermute | solution.py:161
  29.4 0.3 shard_map.68.refs_3_
  29.7 0.0 collective-permute-done.4.refs_2_.tb_ref
  29.7 1.4 %shard_map.69.refs_4_ = f32[4,128]{1,0:T(4,128)S(1)} custom-call(bf16[512,256]{1,0:T(8,128)(2,1)S(1)} %bitcast.11, bf16[1024,256]{1,0:T(8,128)(2,1)S(1)} %constant_dynamic-update-slice_fusion.refs_1_.ta_ref, bf16[1024,256]{1,0:T(8,128)(2,1)S(1)} %collective-permute-done.4.refs_2_.tb_ref, f32[2048,128]{1,0:T(8,128)S(1)} %shard_map.68.refs_3_), custom_call_target="tpu_custom_call" | custom-call | flops 536870912 | bytes 8388608 | tf_op jit(solution)/shard_map/pallas_call | solution.py:177
  31.1 1.4 %shard_map.71.refs_6_ = f32[4,128]{1,0:T(4,128)S(1)} custom-call(bf16[512,256]{1,0:T(8,128)(2,1)S(1)} %collective-permute-done.6.refs_0_.s2, bf16[1024,256]{1,0:T(8,128)(2,1)S(1)} %constant_dynamic-update-slice_fusion.refs_1_.ta_ref, bf16[1024,256]{1,0:T(8,128)(2,1)S(1)} %collective-permute-done.4.refs_2_.tb_ref, f32[2048,128]{1,0:T(8,128)S(1)} %shard_map.68.refs_3_), custom_call_target="tpu_custom_call" | custom-call | flops 536870912 | bytes 8388608 | tf_op jit(solution)/shard_map/pallas_call | solution.py:177
  32.5 5.1 %collective-permute-done.5.refs_0_.s1 = bf16[512,256]{1,0:T(8,128)(2,1)S(1)} collective-permute-done((bf16[512,256]{1,0:T(8,128)(2,1)S(1)}, bf16[512,256]{1,0:T(8,128)(2,1)S(1)}, u32[]{:S(2)}, u32[]{:S(2)}) %collective-permute-start.5) | collective-permute-done | bytes 262176 | tf_op jit(solution)/shard_map/ppermute | solution.py:161
  37.6 1.4 %shard_map.70.refs_5_ = f32[4,128]{1,0:T(4,128)S(1)} custom-call(bf16[512,256]{1,0:T(8,128)(2,1)S(1)} %collective-permute-done.5.refs_0_.s1, bf16[1024,256]{1,0:T(8,128)(2,1)S(1)} %constant_dynamic-update-slice_fusion.refs_1_.ta_ref, bf16[1024,256]{1,0:T(8,128)(2,1)S(1)} %collective-permute-done.4.refs_2_.tb_ref, f32[2048,128]{1,0:T(8,128)S(1)} %shard_map.68.refs_3_), custom_call_target="tpu_custom_call" | custom-call | flops 536870912 | bytes 8388608 | tf_op jit(solution)/shard_map/pallas_call | solution.py:177
  39.0 0.0 collective-permute-done.refs_0_.s3
  39.0 2.1 %shard_map.72 = f32[32,16,128]{2,1,0:T(8,128)} custom-call(bf16[512,256]{1,0:T(8,128)(2,1)S(1)} %collective-permute-done.refs_0_.s3, bf16[1024,256]{1,0:T(8,128)(2,1)S(1)} %constant_dynamic-update-slice_fusion.refs_1_.ta_ref, bf16[1024,256]{1,0:T(8,128)(2,1)S(1)} %collective-permute-done.4.refs_2_.tb_ref, f32[2048,128]{1,0:T(8,128)S(1)} %shard_map.68.refs_3_, ...), custom_call_target="tpu_custom_call" | custom-call | flops 536870912 | bytes 8388608 | tf_op jit(solution)/shard_map/pallas_call | solution.py:187
  41.1 5.7 %all-to-all-start.1 = ((f32[32,16,128]{2,1,0:T(8,128)}), f32[32,16,128]{2,1,0:T(8,128)S(1)}, u32[]{:S(2)}, u32[]{:S(2)}) async-start(f32[32,16,128]{2,1,0:T(8,128)} %shard_map.72), calls=%async_computation.1 | async-start | bytes 524288 | tf_op jit(solution)/shard_map/all_to_all | solution.py:196
  46.8 0.1 reshape.31
  46.9 0.1 reshape.32.sw_ref
  47.0 10.1 %all-to-all-done.1.got_ref = f32[32,16,128]{2,1,0:T(8,128)S(1)} async-done(((f32[32,16,128]{2,1,0:T(8,128)}), f32[32,16,128]{2,1,0:T(8,128)S(1)}, u32[]{:S(2)}, u32[]{:S(2)}) %all-to-all-start.1) | async-done | bytes 262176 | tf_op jit(solution)/shard_map/all_to_all | solution.py:196
  57.0 7.2 %shard_map.73 = (f32[8,16,128]{2,1,0:T(8,128)}, f32[16,128]{1,0:T(8,128)S(1)}) custom-call(f32[32,16,128]{2,1,0:T(8,128)S(1)} %all-to-all-done.1.got_ref, f32[16,128]{1,0:T(8,128)S(1)} %reshape.32.sw_ref, bf16[512,256]{1,0:T(8,128)(2,1)S(1)} %bitcast.12, bf16[512,256]{1,0:T(8,128)(2,1)S(1)} %collective-permute-done.5.refs_0_.s1, ...), custom_call_target="tpu_custom_call" | custom-call | flops 2147483648 | bytes 8388608 | tf_op jit(solution)/shard_map/pallas_call | solution.py:200
  64.2 9.6 %all-to-all-start.2 = ((f32[8,16,128]{2,1,0:T(8,128)}), f32[8,16,128]{2,1,0:T(8,128)S(1)}, u32[]{:S(2)}, u32[]{:S(2)}) async-start(f32[8,16,128]{2,1,0:T(8,128)} %get-tuple-element.5), calls=%async_computation.2 | async-start | bytes 131072 | tf_op jit(solution)/shard_map/all_to_all | solution.py:213
  73.9 0.1 reshape.33
  74.0 0.7 reshape.34
  74.6 4.1 %all-to-all-done.2.got_ref = f32[8,16,128]{2,1,0:T(8,128)S(1)} async-done(((f32[8,16,128]{2,1,0:T(8,128)}), f32[8,16,128]{2,1,0:T(8,128)S(1)}, u32[]{:S(2)}, u32[]{:S(2)}) %all-to-all-start.2) | async-done | bytes 65568 | tf_op jit(solution)/shard_map/all_to_all | solution.py:213
  78.7 0.6 shard_map.74
  (14 shorter events, 0.1 us)
Async XLA Ops:
  0.6 14.9 %collective-permute-start.1 = (bf16[256,256]{1,0:T(8,128)(2,1)}, bf16[256,256]{1,0:T(8,128)(2,1)S(1)}, u32[]{:S(2)}, u32[]{:S(2)}) collective-permute-start(bf16[256,256]{1,0:T(8,128)(2,1)} %param.6), channel_id=1, source_target_pairs={{0,64},{64,128},{128,192},{192,0},{1,65},{65,129},{129,193},{193,1... | collective-permute-start | bytes 393224 | tf_op jit(solution)/shard_map/ppermute | solution.py:156
  2.7 12.8 %collective-permute-start.2 = (bf16[256,256]{1,0:T(8,128)(2,1)}, bf16[256,256]{1,0:T(8,128)(2,1)S(1)}, u32[]{:S(2)}, u32[]{:S(2)}) collective-permute-start(bf16[256,256]{1,0:T(8,128)(2,1)} %param.6), channel_id=1, source_target_pairs={{0,192},{64,0},{128,64},{192,128},{1,193},{65,1},{129,65},{193,129... | collective-permute-start | bytes 393224 | tf_op jit(solution)/shard_map/ppermute | solution.py:156
  4.1 11.5 %collective-permute-start.3 = (bf16[256,256]{1,0:T(8,128)(2,1)}, bf16[256,256]{1,0:T(8,128)(2,1)S(1)}, u32[]{:S(2)}, u32[]{:S(2)}) collective-permute-start(bf16[256,256]{1,0:T(8,128)(2,1)} %param.6), channel_id=1, source_target_pairs={{0,128},{64,192},{128,0},{192,64},{1,129},{65,193},{129,1},{193,65... | collective-permute-start | bytes 393224 | tf_op jit(solution)/shard_map/ppermute | solution.py:156
  7.2 8.3 %copy-start.2 = (bf16[256,256]{1,0:T(8,128)(2,1)S(1)}, bf16[256,256]{1,0:T(8,128)(2,1)}, u32[]{:S(2)}) copy-start(bf16[256,256]{1,0:T(8,128)(2,1)} %param.6) | copy-start | bytes 393220
  7.2 17.8 %all-to-all-start = ((bf16[8,64,256]{2,1,0:T(8,128)(2,1)}), bf16[8,64,256]{2,1,0:T(8,128)(2,1)S(1)}, u32[]{:S(2)}, u32[]{:S(2)}) async-start(bf16[8,64,256]{2,1,0:T(8,128)(2,1)} %broadcast_in_dim.2), calls=%async_computation | async-start | bytes 524288 | tf_op jit(solution)/shard_map/all_to_all | solution.py:159
  15.6 13.8 %copy-start = (f32[2048]{0:T(1024)S(1)}, f32[2048]{0:T(1024)}, u32[]{:S(2)}) copy-start(f32[2048]{0:T(1024)} %param.9) | copy-start | bytes 24580
  15.7 14.1 %collective-permute-start.4 = (bf16[1024,256]{1,0:T(8,128)(2,1)S(1)}, bf16[1024,256]{1,0:T(8,128)(2,1)S(1)}, u32[]{:S(2)}, u32[]{:S(2)}) collective-permute-start(bf16[1024,256]{1,0:T(8,128)(2,1)S(1)} %constant_dynamic-update-slice_fusion.refs_1_.ta_ref), channel_id=1, source_target_pairs={{0,32},{32,0},{1,33},{33,1},{2,34},{34,2},{3,35},{35,3},{4,36},{36... | collective-permute-start | bytes 1572872 | tf_op jit(solution)/shard_map/ppermute | solution.py:158
  25.0 6.1 %collective-permute-start.6 = (bf16[512,256]{1,0:T(8,128)(2,1)S(1)}, bf16[512,256]{1,0:T(8,128)(2,1)S(1)}, u32[]{:S(2)}, u32[]{:S(2)}) collective-permute-start(bf16[512,256]{1,0:T(8,128)(2,1)S(1)} %bitcast.8), channel_id=1, source_target_pairs={{0,3},{1,0},{2,1},{3,2},{4,7},{5,4},{6,5},{7,6},{8,11},{9,8},{10,9... | collective-permute-start | bytes 786440 | tf_op jit(solution)/shard_map/ppermute | solution.py:161
  27.8 9.9 %collective-permute-start.5 = (bf16[512,256]{1,0:T(8,128)(2,1)S(1)}, bf16[512,256]{1,0:T(8,128)(2,1)S(1)}, u32[]{:S(2)}, u32[]{:S(2)}) collective-permute-start(bf16[512,256]{1,0:T(8,128)(2,1)S(1)} %bitcast.9), channel_id=1, source_target_pairs={{0,1},{1,2},{2,3},{3,0},{4,5},{5,6},{6,7},{7,4},{8,9},{9,10},{10,1... | collective-permute-start | bytes 786440 | tf_op jit(solution)/shard_map/ppermute | solution.py:161
  27.8 11.3 %collective-permute-start = (bf16[512,256]{1,0:T(8,128)(2,1)S(1)}, bf16[512,256]{1,0:T(8,128)(2,1)S(1)}, u32[]{:S(2)}, u32[]{:S(2)}) collective-permute-start(bf16[512,256]{1,0:T(8,128)(2,1)S(1)} %bitcast.10), channel_id=1, source_target_pairs={{0,2},{1,3},{2,0},{3,1},{4,6},{5,7},{6,4},{7,5},{8,10},{9,11},{10,... | collective-permute-start | bytes 786440 | tf_op jit(solution)/shard_map/ppermute | solution.py:161
  41.1 5.7 %copy-start.3 = (f32[2048]{0:T(1024)S(1)}, f32[2048]{0:T(1024)}, u32[]{:S(2)}) copy-start(f32[2048]{0:T(1024)} %param.7) | copy-start | bytes 24580
  41.1 15.9 %all-to-all-start.1 = ((f32[32,16,128]{2,1,0:T(8,128)}), f32[32,16,128]{2,1,0:T(8,128)S(1)}, u32[]{:S(2)}, u32[]{:S(2)}) async-start(f32[32,16,128]{2,1,0:T(8,128)} %shard_map.72), calls=%async_computation.1 | async-start | bytes 524288 | tf_op jit(solution)/shard_map/all_to_all | solution.py:196
  64.2 14.5 %all-to-all-start.2 = ((f32[8,16,128]{2,1,0:T(8,128)}), f32[8,16,128]{2,1,0:T(8,128)S(1)}, u32[]{:S(2)}, u32[]{:S(2)}) async-start(f32[8,16,128]{2,1,0:T(8,128)} %get-tuple-element.5), calls=%async_computation.2 | async-start | bytes 131072 | tf_op jit(solution)/shard_map/all_to_all | solution.py:213
  74.0 4.8 %copy-start.1 = (f32[2048]{0:T(1024)S(1)}, f32[2048]{0:T(1024)}, u32[]{:S(2)}) copy-start(f32[2048]{0:T(1024)} %param.8) | copy-start | bytes 24580

commit v2 on v0

v2 whole, which is shorter than its diff:
```python
import functools
import math

import jax
import jax.numpy as jnp
from jax import lax
from jax.experimental import pallas as pl
from jax.experimental.pallas import tpu as pltpu
from jax.sharding import Mesh
from jax.sharding import PartitionSpec as P

EPSILON = 0.25
LANES = 128
STRIP = 256
STEP = 64
NX, NC, NZ, NY = 4, 2, 8, 4
SHIFTS = (0, 1, 3, 2)
SAFE = 2.0**-90
VMEM = pl.BlockSpec(memory_space=pltpu.VMEM)
MIB = 1024 * 1024
f32 = jnp.float32


def params(mib):
    return pltpu.CompilerParams(vmem_limit_bytes=mib * MIB)


def contract(a, b):
    return lax.dot_general(a, b, (((1,), (1,)), ((), ())), preferred_element_type=f32)


def spread(row):
    return jnp.broadcast_to(row, (LANES, LANES)).T


def spread_rows(rows_of, count, out):
    for n in range(count):
        out[n * LANES : (n + 1) * LANES, :] = spread(rows_of(n))


def halves():
    return [(h, slice(h * LANES, (h + 1) * LANES)) for h in range(STRIP // LANES)]


def add_and_top(buf, bias, base, lanes):
    top = None
    for r in range(0, buf.shape[0], STEP):
        value = buf[r : r + STEP, lanes] + bias[base + r : base + r + STEP, :]
        buf[r : r + STEP, lanes] = value
        top = value if top is None else jnp.maximum(top, value)
    return jnp.max(top, axis=0, keepdims=True)


def sum_exp(buf, top, lanes, rate):
    total = None
    for r in range(0, buf.shape[0], STEP):
        value = jnp.exp2((buf[r : r + STEP, lanes] - top) * rate)
        total = value if total is None else total + value
    return jnp.sum(total, axis=0, keepdims=True)


def lse_of(buf, bias, rate, base=0):
    out = []
    for _, lanes in halves():
        top = add_and_top(buf, bias, base, lanes)
        out.append(top + jnp.log2(sum_exp(buf, top, lanes, rate)) / rate)
    return out


def lse_parts(parts, rate):
    top = jnp.max(parts, axis=0)
    total = jnp.sum(jnp.exp2((parts - top[None]) * rate), axis=0)
    return top + jnp.log2(total) / rate


def all_strips(count, fill, finish, buf0, buf1):
    fill(0, buf0)

    def pair(p, _):
        fill(2 * p + 1, buf1)
        finish(2 * p, buf0)
        fill(jnp.minimum(2 * p + 2, count - 2), buf0)
        finish(2 * p + 1, buf1)
        return 0

    lax.fori_loop(0, count // 2, pair, 0)


def shift_of(n):
    return jnp.where(n == 2, 3, jnp.where(n == 3, 2, n))


def join_kernel(scale, own_ref, pair_ref, gate_ref, *refs):
    del gate_ref
    *pieces, near_ref, bias_ref = refs
    at = 0
    for piece in pieces:
        near_ref[at : at + piece.shape[0], :] = piece[...]
        at += piece.shape[0]
    x, c = lax.axis_index("x"), lax.axis_index("c")
    row = 0
    for other in range(NC):
        for ref in (own_ref, pair_ref):
            for k in SHIFTS:
                block = lax.rem(x - k + NX, NX) * NC + lax.rem(c + other, NC)
                for half in range(2):
                    values = ref[pl.ds(block * 2 + half, 1), :] * (1.0 / scale)
                    bias_ref[row * LANES : (row + 1) * LANES, :] = spread(values)
                    row += 1


def products(s_ref, t_ref, bufs):
    for n, buf in enumerate(bufs):
        buf[...] = contract(t_ref[...], s_ref[n * STRIP : (n + 1) * STRIP, :])


def row_first(rate, s_ref, t_ref, bias_ref, out_ref, buf0, buf1):
    products(s_ref, t_ref, (buf0, buf1))
    out_ref[...] = jnp.concatenate(lse_of(buf0, bias_ref, rate) + lse_of(buf1, bias_ref, rate), axis=0)


def row_second(rate, s_ref, t_ref, bias_ref, first_ref, out_ref, buf0, buf1):
    products(s_ref, t_ref, (buf0, buf1))
    base = t_ref.shape[0]
    mine = jnp.concatenate(lse_of(buf0, bias_ref, rate, base) + lse_of(buf1, bias_ref, rate, base), axis=0)
    out_ref[...] = lse_parts(jnp.stack([first_ref[...], mine]), rate)


def row_third(rate, s_ref, ta_ref, tb_ref, bias_ref, own_ref, out_ref, rows_ref, buf0, buf1, buf2, buf3):
    products(s_ref, ta_ref, (buf0, buf1))
    products(s_ref, tb_ref, (buf2, buf3))
    base = ta_ref.shape[0]
    near = jnp.concatenate(lse_of(buf0, bias_ref, rate) + lse_of(buf1, bias_ref, rate), axis=0)
    far = jnp.concatenate(lse_of(buf2, bias_ref, rate, base) + lse_of(buf3, bias_ref, rate, base), axis=0)
    pair = lse_parts(jnp.stack([near, far]), rate)
    own = own_ref[...]
    low = lax.rem(lax.axis_index("y"), 2) == 0
    rows = jnp.concatenate([jnp.where(low, own, pair), jnp.where(low, pair, own)], axis=0)
    rows_ref[...] = rows
    out_ref[...] = jnp.broadcast_to(rows[None], out_ref.shape)


def row_order(scratch):
    half = scratch.shape[0] // 2
    own = lax.rem(lax.axis_index("y"), 2)

    def row(n):
        at = jnp.where(own == n // half, 0, half)
        return scratch[pl.ds(at + n % half, 1), :]

    return row


def fill_strip(t_ref, sources):
    def fill(n, buf):
        strip = t_ref[pl.ds(pl.multiple_of(n * STRIP, STRIP), STRIP), :]
        at = 0
        for s_ref in sources:
            buf[at : at + s_ref.shape[0], :] = contract(s_ref[...], strip)
            at += s_ref.shape[0]

    return fill


def swap_halves(even, odd):
    low = lax.broadcasted_iota(jnp.int32, even.shape, 1) < LANES // 2
    turn = functools.partial(pltpu.roll, shift=LANES // 2, axis=1)
    return jnp.where(low, even, turn(odd)), jnp.where(low, turn(even), odd)


def fold(value, op):
    out = value[:STEP]
    for r in range(STEP, value.shape[0], STEP):
        out = op(out, value[r : r + STEP])
    return out


def over_strip(sources, bias, strip, each, op):
    got = [None] * (STRIP // LANES)
    at = 0
    for s_ref in sources:
        for r in range(0, s_ref.shape[0], STRIP):
            product = contract(s_ref[r : r + STRIP, :], strip)
            for h, lanes in halves():
                value = fold(each(h, product[:, lanes] + bias[at : at + STRIP, :]), op)
                got[h] = value if got[h] is None else op(got[h], value)
            at += STRIP
    return got


def strips_of(*targets):
    strip = 0
    for t_ref in targets:
        for r in range(0, t_ref.shape[0], STRIP):
            yield strip, t_ref[r : r + STRIP, :]
            strip += 1


def early_kernel(rate, scale, offset, rows_ref, sw_ref, s0, s1, ta_ref, tb_ref, top_ref, ready_ref, bias, ahead):
    high = lax.axis_index("y") // 2
    rows = [sw_ref[pl.ds(2 * z + high, 1), :] for z in range(NZ)]
    weight = jnp.concatenate(swap_halves(jnp.concatenate(rows[0::2], axis=0), jnp.concatenate(rows[1::2], axis=0)), axis=0)
    ready = (jnp.log(weight) + offset) * (1.0 / scale)
    ready_ref[...] = ready
    ahead[...] = ready - rows_ref[...]
    spread_rows(row_order(ahead), bias.shape[0] // LANES, bias)
    for n, strip in strips_of(ta_ref, tb_ref):
        tops = over_strip((s0, s1), bias, strip, lambda h, value: value, jnp.maximum)
        for h, top in enumerate(tops):
            top_ref[2 * n + h : 2 * n + h + 1, :] = jnp.max(top, axis=0, keepdims=True)


def col_kernel(rate, got_ref, rows_ref, ready_ref, top_ref, s0, s1, ta_ref, tb_ref, out_ref, buf0, buf1, bias, ahead, cols, worst):
    lse = lse_parts(got_ref[...], rate)
    potential = ready_ref[...] - lse
    least = jnp.min(lse - rows_ref[...])
    ahead[...] = potential
    spread_rows(row_order(ahead), bias.shape[0] // LANES, bias)
    count = ta_ref.shape[0] // STRIP
    x, c, y = lax.axis_index("x"), lax.axis_index("c"), lax.axis_index("y")
    mine = jnp.where(y >= 2, 1, 0)

    def put(strip, values):
        core = lax.rem(c + strip // count, NC)
        at = lax.rem(strip, count)
        block = lax.rem(x - shift_of(lax.rem(at, NX)) + NX, NX) * NC + core
        side = jnp.where(at < NX, mine, 1 - mine)
        for h, value in enumerate(values):
            cols[side, pl.ds(block * 2 + h, 1), :] = value

    low = None
    for n, strip in strips_of(ta_ref, tb_ref):
        tops = [top_ref[2 * n + h : 2 * n + h + 1, :] - least for h in range(STRIP // LANES)]
        parts = over_strip((s0, s1), bias, strip, lambda h, value: jnp.exp2((value - tops[h]) * rate), jnp.add)
        totals = [jnp.sum(part, axis=0, keepdims=True) for part in parts]
        for total in totals:
            low = total if low is None else jnp.minimum(low, total)
        put(jnp.int32(n), [top + jnp.log2(total) / rate for top, total in zip(tops, totals)])
    worst[...] = low

    @pl.when(jnp.logical_not(jnp.min(worst[...]) >= SAFE))
    def _():
        for other, t_ref in enumerate((ta_ref, tb_ref)):

            def finish(n, buf, other=other):
                put(other * count + n, lse_of(buf, bias, rate))

            all_strips(count, fill_strip(t_ref, (s0, s1)), finish, buf0, buf1)

    for n in range(out_ref.shape[0]):
        out_ref[n, : cols.shape[1], :] = cols[n % 2]
        out_ref[n, cols.shape[1] :, :] = potential


def last_kernel(rate, scale, offset, got_ref, tw_ref, sp_ref, out_ref):
    n_cols = tw_ref.shape[0]
    out_ref[...] = jnp.log(tw_ref[...]) - (lse_parts(got_ref[:, :n_cols, :], rate) * scale - offset)
    place = 2 * (lax.axis_index("x") * NC + lax.axis_index("c"))
    for n in range(2):
        rows = got_ref[place + n, n_cols:, :] * scale
        half = rows.shape[0] // 2
        for odd, part in enumerate(swap_halves(rows[:half], rows[half:])):
            for j in range(half):
                at = 4 * j + 2 * odd + n
                sp_ref[at : at + 1, :] = part[j : j + 1, :]


def cost(mib, flops=0):
    return pl.CostEstimate(flops=int(flops), bytes_accessed=int(mib * MIB), transcendentals=0)


def per_device(source_points, target_points, source_weight, target_weight, target_potential):
    width = source_points.shape[1]
    scale = 1.0 / (EPSILON * math.sqrt(width))
    rate = scale * math.log2(math.e)
    n_rows, n_cols = source_weight.shape[0], target_weight.shape[0]
    rows_all, cols_all = n_rows * NX * NC, n_cols * NZ * NY
    half_rows = n_rows // 2

    def around(n, k):
        return [(i, (i + k) % n) for i in range(n)]

    beside = [(i, i ^ 1) for i in range(NY)]
    across = [(i, i ^ 3) for i in range(NY)]
    z_beside = [[z * NY + y for z in range(NZ) for y in p] for p in ((0, 1), (2, 3))]
    xc_across = [[n * NY + y for n in range(NX * NC) for y in p] for p in ((0, 3), (1, 2))]

    potential = target_potential.reshape(-1, LANES)
    copies = jnp.broadcast_to(source_points[None], (NZ,) + source_points.shape)
    pair_points = lax.ppermute(target_points, "y", across)
    pair_potential = lax.ppermute(potential, "y", across)
    pieces = [lax.ppermute(points, "x", around(NX, k)) if k else points for points in (target_points, pair_points) for k in SHIFTS]
    own = lax.all_to_all(copies, "z", 0, 0).reshape(-1, width)
    block = len(pieces) * target_points.shape[0]
    near, bias = pl.pallas_call(
        functools.partial(join_kernel, scale),
        out_shape=[jax.ShapeDtypeStruct((block, width), jnp.bfloat16), jax.ShapeDtypeStruct((2 * block, LANES), f32)],
        in_specs=[VMEM, VMEM, pl.BlockSpec(memory_space=pl.ANY)] + [VMEM] * len(pieces),
        out_specs=[VMEM] * 2,
        compiler_params=params(16),
        cost_estimate=cost(8),
    )(potential, pair_potential, own, *pieces)
    far = lax.ppermute(near, "c", around(NC, 1))
    pair = lax.ppermute(own, "y", beside)
    chunk = own.shape[0]
    sub = half_rows // LANES

    buf = pltpu.VMEM((block, STRIP), f32)
    part = jax.ShapeDtypeStruct((chunk // LANES, LANES), f32)
    first = pl.pallas_call(
        functools.partial(row_first, rate),
        out_shape=part,
        in_specs=[VMEM] * 3,
        out_specs=VMEM,
        scratch_shapes=[buf] * 2,
        compiler_params=params(16),
        cost_estimate=cost(1, 4e10),
    )(own, near, bias)
    second = pl.pallas_call(
        functools.partial(row_second, rate),
        out_shape=part,
        in_specs=[VMEM] * 4,
        out_specs=VMEM,
        scratch_shapes=[buf] * 2,
        compiler_params=params(16),
        cost_estimate=cost(0.25),
    )(own, far, bias, first)
    sent, rows = pl.pallas_call(
        functools.partial(row_third, rate),
        out_shape=[jax.ShapeDtypeStruct((2 * NZ, sub, LANES), f32), jax.ShapeDtypeStruct((sub, LANES), f32)],
        in_specs=[VMEM] * 5,
        out_specs=[VMEM] * 2,
        scratch_shapes=[buf] * 4,
        compiler_params=params(16),
        cost_estimate=cost(16),
    )(pair, near, far, bias, second)
    got = lax.all_to_all(sent, ("z", "y"), 0, 0, axis_index_groups=z_beside)

    strips = 2 * block // STRIP
    held = [pltpu.VMEM((half_rows, LANES), f32), pltpu.VMEM((sub, LANES), f32)]
    tops, ready = pl.pallas_call(
        functools.partial(early_kernel, rate, scale, math.log(cols_all)),
        out_shape=[jax.ShapeDtypeStruct((2 * strips, LANES), f32), jax.ShapeDtypeStruct((sub, LANES), f32)],
        in_specs=[VMEM] * 6,
        out_specs=[VMEM] * 2,
        scratch_shapes=held,
        compiler_params=params(16),
        cost_estimate=cost(16),
    )(rows, source_weight.reshape(-1, LANES), own, pair, near, far)
    sent = pl.pallas_call(
        functools.partial(col_kernel, rate),
        out_shape=jax.ShapeDtypeStruct((2 * NX * NC, n_cols // LANES + sub, LANES), f32),
        in_specs=[VMEM] * 8,
        out_specs=VMEM,
        scratch_shapes=[pltpu.VMEM((half_rows, STRIP), f32)] * 2 + held + [pltpu.VMEM((2, n_cols // LANES, LANES), f32), pltpu.VMEM((1, LANES), f32)],
        compiler_params=params(16),
        cost_estimate=cost(16),
    )(got, rows, ready, tops, own, pair, near, far)
    got = lax.all_to_all(sent, ("x", "c", "y"), 0, 0, axis_index_groups=xc_across)
    potential, updated = pl.pallas_call(
        functools.partial(last_kernel, rate, scale, math.log(rows_all)),
        out_shape=[jax.ShapeDtypeStruct((n // LANES, LANES), f32) for n in (n_rows, n_cols)],
        in_specs=[VMEM] * 2,
        out_specs=[VMEM] * 2,
        compiler_params=params(16),
    )(got, target_weight.reshape(-1, LANES))
    return potential.reshape(-1), updated.reshape(-1)


def solution(mesh):
    grid = Mesh(mesh.devices.reshape(NX, NC, NZ, NY), ("x", "c", "z", "y"))
    return jax.shard_map(
        per_device,
        mesh=grid,
        in_specs=(P(("x", "c", "z", "y"), None), P(("z", "y", "x", "c"), None), P(("x", "c")), P(("z", "y")), P(("z", "y"))),
        out_specs=(P(("x", "c")), P(("z", "y"))),
        check_vma=False,
    )
```

time: 332 us -> 81.6 us (0.25)
  blocking collectives: 174 us -> 14.5 us
  waiting for transfers between devices: 107 us -> 14.9 us
  starting transfers between devices: 0.08 us -> 27.6 us
  matrix products: 20.5 us -> 0 us
  Pallas kernels: 0 us -> 20.5 us
  other arithmetic: 15.4 us -> 0 us
  between operations: 14.2 us -> 0.71 us
    all_gather x2 -> x0, waiting for transfers between devices: 105 us -> none  [the longest x1 73.9 us: per_device(): sources = lax.all_gather(source_points, 'col', axis=0, tiled=True)]
    pmax x2 -> x0, blocking collectives: 104 us -> none  [the longest x1 59 us: per_device(): global_max = lax.pmax(row_max, 'col')]
    psum x2 -> x0, blocking collectives: 69.6 us -> none  [the longest x1 56.9 us: per_device(): row_total = lax.psum(row_total * jnp.exp(row_max - global_max), 'col')]
    pallas_call x0 -> x7, Pallas kernels: none -> 20.5 us  [the longest x1 10.6 us: per_device(): pl.pallas_call(functools.partial(col_kernel, rate), out_shape=jax.ShapeDt...]
    dot_general x5 -> x0, matrix products: 20.5 us -> none  [the longest x4 10.8 us: per_device(): jnp.einsum('id,jd->ij', sources[first_row:first_row + block_rows], shard_...]
    all_to_all x0 -> x2, starting transfers between devices: none -> 15.9 us  [the longest x1 9.01 us: per_device(): own = lax.all_to_all(copies, 'z', 0, 0).reshape(-1, width)]
    reduce_sum x3 -> x0, other arithmetic: 14.7 us -> none  [the longest x1 8.13 us: update_rows(): totals = jnp.sum(jnp.exp(logits - highest[:, None]), axis=1)]
    all_to_all x0 -> x1, blocking collectives: none -> 14.5 us  [per_device(): lax.all_to_all(sent, ('x', 'c', 'y'), 0, 0, axis_index_groups=xc_across)]
  transfers between devices with their start and end apart: 2 -> 12, of which waited for: 2 -> 7; matrix products, arithmetic and copies ran while one was open for 0% -> 0% of each run, Pallas kernels for 0% -> 7%
where the time goes in v2:
time: 81.6 us; the launch traced here: 81.2 us
  starting transfers between devices  27.6 us (34%)
  Pallas kernels  20.5 us (25%)
  waiting for transfers between devices  14.9 us (18%)
  blocking collectives  14.5 us (18%)
  local copies, waits for them, and re-layouts  3.08 us (4%)
    all_to_all x1, blocking collectives, per_device(): lax.all_to_all(sent, ('x', 'c', 'y'), 0, 0, axis_index_groups=xc_across)  14.5 us
    pallas_call x1, Pallas kernels, per_device(): pl.pallas_call(functools.partial(col_kernel, rate), out_shape=jax.ShapeDt...  10.6 us
    all_to_all x1, starting transfers between devices, per_device(): own = lax.all_to_all(copies, 'z', 0, 0).reshape(-1, width)  9.01 us
    all_to_all x1, starting transfers between devices, per_device(): got = lax.all_to_all(sent, ('z', 'y'), 0, 0, axis_index_groups=z_beside)  6.92 us
    ppermute x6, waiting for transfers between devices, per_device(): lax.ppermute(points, 'x', around(NX, k))  6.83 us
    ppermute x6, starting transfers between devices, per_device(): lax.ppermute(points, 'x', around(NX, k))  6.67 us
    all_to_all x1, waiting for transfers between devices, per_device(): got = lax.all_to_all(sent, ('z', 'y'), 0, 0, axis_index_groups=z_beside)  5.45 us
    pallas_call x1, Pallas kernels, per_device(): pl.pallas_call(functools.partial(row_third, rate), out_shape=[jax.ShapeDt...  3.42 us
  transfers between devices with their start and end apart: 12, of which 7 were waited for; matrix products, arithmetic and copies ran while one was open for 0% of the time, Pallas kernels for 7%

profile of v2, /device:TPU:1, one launch (start us, length us, event | category | flops | bytes accessed | tf_op | source)
XLA Modules:
  0.0 81.2 jit_solution(3779111632994024390)
XLA Ops:
  0.6 1.5 %broadcast_in_dim.2 = bf16[8,64,256]{2,1,0:T(8,128)(2,1)} broadcast(bf16[64,256]{1,0:T(8,128)(2,1)} %param.5), dimensions={1,2} | broadcast | bytes 294912 | tf_op jit(solution)/shard_map/broadcast_in_dim | solution.py:289
  2.1 9.0 %all-to-all-start = ((bf16[8,64,256]{2,1,0:T(8,128)(2,1)}), bf16[8,64,256]{2,1,0:T(8,128)(2,1)S(1)}, u32[]{:S(2)}, u32[]{:S(2)}) async-start(bf16[8,64,256]{2,1,0:T(8,128)(2,1)} %broadcast_in_dim.2), calls=%async_computation | async-start | bytes 524288 | tf_op jit(solution)/shard_map/all_to_all | solution.py:293
  11.1 2.7 %collective-permute-start.5 = (bf16[256,256]{1,0:T(8,128)(2,1)}, bf16[256,256]{1,0:T(8,128)(2,1)S(1)}, u32[]{:S(2)}, u32[]{:S(2)}) collective-permute-start(bf16[256,256]{1,0:T(8,128)(2,1)} %refs_0_.1), channel_id=1, source_target_pairs={{0,3},{1,2},{2,1},{3,0},{4,7},{5,6},{6,5},{7,4},{8,11},{9,10},{10,... | collective-permute-start | bytes 393224 | tf_op jit(solution)/shard_map/ppermute | solution.py:290
  13.8 2.7 %collective-permute-start.4 = (bf16[256,256]{1,0:T(8,128)(2,1)}, bf16[256,256]{1,0:T(8,128)(2,1)S(1)}, u32[]{:S(2)}, u32[]{:S(2)}) collective-permute-start(bf16[256,256]{1,0:T(8,128)(2,1)} %refs_0_.1), channel_id=1, source_target_pairs={{0,128},{64,192},{128,0},{192,64},{1,129},{65,193},{129,1},{193,65... | collective-permute-start | bytes 393224 | tf_op jit(solution)/shard_map/ppermute | solution.py:292
  16.6 0.1 collective-permute-start.1
  16.7 0.9 %collective-permute-start.3 = (bf16[256,256]{1,0:T(8,128)(2,1)}, bf16[256,256]{1,0:T(8,128)(2,1)S(1)}, u32[]{:S(2)}, u32[]{:S(2)}) collective-permute-start(bf16[256,256]{1,0:T(8,128)(2,1)} %refs_0_.1), channel_id=1, source_target_pairs={{0,192},{64,0},{128,64},{192,128},{1,193},{65,1},{129,65},{193,129... | collective-permute-start | bytes 393224 | tf_op jit(solution)/shard_map/ppermute | solution.py:292
  17.6 0.6 collective-permute-start.2
  18.2 1.0 %collective-permute-start.8 = (bf16[256,256]{1,0:T(8,128)(2,1)S(1)}, bf16[256,256]{1,0:T(8,128)(2,1)S(1)}, u32[]{:S(2)}, u32[]{:S(2)}) collective-permute-start(bf16[256,256]{1,0:T(8,128)(2,1)S(1)} %collective-permute-done.5.refs_4_), channel_id=1, source_target_pairs={{0,128},{64,192},{128,0},{192,64},{1,129},{65,193},{129,1},{193,65... | collective-permute-start | bytes 393224 | tf_op jit(solution)/shard_map/ppermute | solution.py:292
  19.2 1.7 %collective-permute-done.1.pair_ref = f32[16,128]{1,0:T(8,128)S(1)} collective-permute-done((f32[16,128]{1,0:T(8,128)}, f32[16,128]{1,0:T(8,128)S(1)}, u32[]{:S(2)}, u32[]{:S(2)}) %collective-permute-start.1) | collective-permute-done | bytes 8224 | tf_op jit(solution)/shard_map/ppermute | solution.py:291
  20.8 0.9 %collective-permute-start.7 = (bf16[256,256]{1,0:T(8,128)(2,1)S(1)}, bf16[256,256]{1,0:T(8,128)(2,1)S(1)}, u32[]{:S(2)}, u32[]{:S(2)}) collective-permute-start(bf16[256,256]{1,0:T(8,128)(2,1)S(1)} %collective-permute-done.5.refs_4_), channel_id=1, source_target_pairs={{0,192},{64,0},{128,64},{192,128},{1,193},{65,1},{129,65},{193,129... | collective-permute-start | bytes 393224 | tf_op jit(solution)/shard_map/ppermute | solution.py:292
  21.7 0.6 collective-permute-start.6
  22.3 0.5 collective-permute-start
  22.8 0.8 collective-permute-done.2.refs_1_
  23.6 2.3 %collective-permute-done.8.refs_7_ = bf16[256,256]{1,0:T(8,128)(2,1)S(1)} collective-permute-done((bf16[256,256]{1,0:T(8,128)(2,1)S(1)}, bf16[256,256]{1,0:T(8,128)(2,1)S(1)}, u32[]{:S(2)}, u32[]{:S(2)}) %collective-permute-start.8) | collective-permute-done | bytes 131104 | tf_op jit(solution)/shard_map/ppermute | solution.py:292
  25.9 1.9 %collective-permute-done.7.refs_6_ = bf16[256,256]{1,0:T(8,128)(2,1)S(1)} collective-permute-done((bf16[256,256]{1,0:T(8,128)(2,1)S(1)}, bf16[256,256]{1,0:T(8,128)(2,1)S(1)}, u32[]{:S(2)}, u32[]{:S(2)}) %collective-permute-start.7) | collective-permute-done | bytes 131104 | tf_op jit(solution)/shard_map/ppermute | solution.py:292
  27.8 1.8 %collective-permute-done.6.refs_5_ = bf16[256,256]{1,0:T(8,128)(2,1)S(1)} collective-permute-done((bf16[256,256]{1,0:T(8,128)(2,1)S(1)}, bf16[256,256]{1,0:T(8,128)(2,1)S(1)}, u32[]{:S(2)}, u32[]{:S(2)}) %collective-permute-start.6) | collective-permute-done | bytes 131104 | tf_op jit(solution)/shard_map/ppermute | solution.py:292
  29.6 0.9 %copy-done = bf16[256,256]{1,0:T(8,128)(2,1)S(1)} copy-done((bf16[256,256]{1,0:T(8,128)(2,1)S(1)}, bf16[256,256]{1,0:T(8,128)(2,1)}, u32[]{:S(2)}) %copy-start) | copy-done | bytes 131096
  30.5 0.7 copy-done.3
  31.2 0.6 shard_map.68
  31.8 1.6 %collective-permute-start.9 = (bf16[2048,256]{1,0:T(8,128)(2,1)S(1)}, bf16[2048,256]{1,0:T(8,128)(2,1)S(1)}, u32[]{:S(2)}, u32[]{:S(2)}) collective-permute-start(bf16[2048,256]{1,0:T(8,128)(2,1)S(1)} %get-tuple-element.10.t_ref.ta_ref), channel_id=1, source_target_pairs={{0,32},{32,0},{1,33},{33,1},{2,34},{34,2},{3,35},{35,3},{4,36},{36... | collective-permute-start | bytes 3145736 | tf_op jit(solution)/shard_map/ppermute | solution.py:303
  33.5 1.4 %shard_map.69.first_ref = f32[4,128]{1,0:T(4,128)S(1)} custom-call(bf16[512,256]{1,0:T(8,128)(2,1)S(1)} %bitcast.8, bf16[2048,256]{1,0:T(8,128)(2,1)S(1)} %get-tuple-element.10.t_ref.ta_ref, f32[4096,128]{1,0:T(8,128)S(1)} %get-tuple-element.11.bias_ref), custom_call_target="tpu_custom_call" | custom-call | flops 40000000000 | bytes 1048576 | tf_op jit(solution)/shard_map/pallas_call | solution.py:310
  34.8 0.9 %collective-permute-done.9.t_ref.tb_ref = bf16[2048,256]{1,0:T(8,128)(2,1)S(1)} collective-permute-done((bf16[2048,256]{1,0:T(8,128)(2,1)S(1)}, bf16[2048,256]{1,0:T(8,128)(2,1)S(1)}, u32[]{:S(2)}, u32[]{:S(2)}) %collective-permute-start.9) | collective-permute-done | bytes 1048608 | tf_op jit(solution)/shard_map/ppermute | solution.py:303
  35.8 1.4 %shard_map.70.own_ref = f32[4,128]{1,0:T(4,128)S(1)} custom-call(bf16[512,256]{1,0:T(8,128)(2,1)S(1)} %bitcast.9, bf16[2048,256]{1,0:T(8,128)(2,1)S(1)} %collective-permute-done.9.t_ref.tb_ref, f32[4096,128]{1,0:T(8,128)S(1)} %get-tuple-element.11.bias_ref, f32[4,128]{1,0:T(4,128)S(1)} %shard_map.69.first_ref), custom_call_target="tpu_custom_call" | custom-call | bytes 262144 | tf_op jit(solution)/shard_map/pallas_call | solution.py:319
  37.1 0.0 copy-start.1
  37.2 3.4 %shard_map.71 = (f32[16,8,128]{2,1,0:T(8,128)}, f32[8,128]{1,0:T(8,128)S(1)}) custom-call(bf16[512,256]{1,0:T(8,128)(2,1)S(1)} %collective-permute-done.s_ref.s1, bf16[2048,256]{1,0:T(8,128)(2,1)S(1)} %get-tuple-element.10.t_ref.ta_ref, bf16[2048,256]{1,0:T(8,128)(2,1)S(1)} %collective-permute-done.9.t_ref.tb_ref, ...), custom_call_target="tpu_custom_call" | custom-call | bytes 16777216 | tf_op jit(solution)/shard_map/pallas_call | solution.py:328
  40.6 6.9 %all-to-all-start.1 = ((f32[16,8,128]{2,1,0:T(8,128)}), f32[16,8,128]{2,1,0:T(8,128)S(1)}, u32[]{:S(2)}, u32[]{:S(2)}) async-start(f32[16,8,128]{2,1,0:T(8,128)} %get-tuple-element.12), calls=%async_computation.1 | async-start | bytes 131072 | tf_op jit(solution)/shard_map/all_to_all | solution.py:337
  47.5 2.4 %shard_map.72 = (f32[32,128]{1,0:T(8,128)S(1)}, f32[8,128]{1,0:T(8,128)S(1)}) custom-call(f32[8,128]{1,0:T(8,128)S(1)} %get-tuple-element.13.rows_ref, f32[16,128]{1,0:T(8,128)S(1)} %bitcast.12, bf16[512,256]{1,0:T(8,128)(2,1)S(1)} %bitcast.10, bf16[512,256]{1,0:T(8,128)(2,1)S(1)} %collective-permute-done.s_ref.s1, ...), custom_call_target="tpu_custom_call" | custom-call | bytes 16777216 | tf_op jit(solution)/shard_map/pallas_call | solution.py:341
  49.9 0.0 copy-start.2
  49.9 5.5 %all-to-all-done.1.got_ref = f32[16,8,128]{2,1,0:T(8,128)S(1)} async-done(((f32[16,8,128]{2,1,0:T(8,128)}), f32[16,8,128]{2,1,0:T(8,128)S(1)}, u32[]{:S(2)}, u32[]{:S(2)}) %all-to-all-start.1) | async-done | bytes 65568 | tf_op jit(solution)/shard_map/all_to_all | solution.py:337
  55.4 10.6 %shard_map.73 = f32[16,24,128]{2,1,0:T(8,128)S(1)} custom-call(f32[16,8,128]{2,1,0:T(8,128)S(1)} %all-to-all-done.1.got_ref, f32[8,128]{1,0:T(8,128)S(1)} %get-tuple-element.13.rows_ref, f32[8,128]{1,0:T(8,128)S(1)} %get-tuple-element.14.ready_ref, f32[32,128]{1,0:T(8,128)S(1)} %get-tuple-element.15.top_ref, bf16[512,256]{1,0:T(8,128)(2,1)S(1)} %bitcast.11, ...), custom_call_target="tpu_custom_call" | custom-call | bytes 16777216 | tf_op jit(solution)/shard_map/pallas_call | solution.py:350
  66.0 14.5 %all_to_all.15.got_ref = f32[16,24,128]{2,1,0:T(8,128)S(1)} all-to-all(f32[16,24,128]{2,1,0:T(8,128)S(1)} %shard_map.73), channel_id=1, replica_groups={{0,3,32,35,64,67,96,99,128,131,160,163,192,195,224,227},{1,2,33,34,65,6..., dimensions={0} | all-to-all | bytes 393216 | tf_op jit(solution)/shard_map/all_to_all | solution.py:359
  80.5 0.7 shard_map.74
  (9 shorter events, 0.0 us)
Async XLA Ops:
  2.1 20.2 %all-to-all-start = ((bf16[8,64,256]{2,1,0:T(8,128)(2,1)}), bf16[8,64,256]{2,1,0:T(8,128)(2,1)S(1)}, u32[]{:S(2)}, u32[]{:S(2)}) async-start(bf16[8,64,256]{2,1,0:T(8,128)(2,1)} %broadcast_in_dim.2), calls=%async_computation | async-start | bytes 524288 | tf_op jit(solution)/shard_map/all_to_all | solution.py:293
  11.1 7.0 %collective-permute-start.5 = (bf16[256,256]{1,0:T(8,128)(2,1)}, bf16[256,256]{1,0:T(8,128)(2,1)S(1)}, u32[]{:S(2)}, u32[]{:S(2)}) collective-permute-start(bf16[256,256]{1,0:T(8,128)(2,1)} %refs_0_.1), channel_id=1, source_target_pairs={{0,3},{1,2},{2,1},{3,0},{4,7},{5,6},{6,5},{7,4},{8,11},{9,10},{10,... | collective-permute-start | bytes 393224 | tf_op jit(solution)/shard_map/ppermute | solution.py:290
  13.8 7.8 %collective-permute-start.4 = (bf16[256,256]{1,0:T(8,128)(2,1)}, bf16[256,256]{1,0:T(8,128)(2,1)S(1)}, u32[]{:S(2)}, u32[]{:S(2)}) collective-permute-start(bf16[256,256]{1,0:T(8,128)(2,1)} %refs_0_.1), channel_id=1, source_target_pairs={{0,128},{64,192},{128,0},{192,64},{1,129},{65,193},{129,1},{193,65... | collective-permute-start | bytes 393224 | tf_op jit(solution)/shard_map/ppermute | solution.py:292
  16.6 4.2 %collective-permute-start.1 = (f32[16,128]{1,0:T(8,128)}, f32[16,128]{1,0:T(8,128)S(1)}, u32[]{:S(2)}, u32[]{:S(2)}) collective-permute-start(f32[16,128]{1,0:T(8,128)} %bitcast.14), channel_id=1, source_target_pairs={{0,3},{1,2},{2,1},{3,0},{4,7},{5,6},{6,5},{7,4},{8,11},{9,10},{10,... | collective-permute-start | bytes 24584 | tf_op jit(solution)/shard_map/ppermute | solution.py:291
  16.7 5.6 %collective-permute-start.3 = (bf16[256,256]{1,0:T(8,128)(2,1)}, bf16[256,256]{1,0:T(8,128)(2,1)S(1)}, u32[]{:S(2)}, u32[]{:S(2)}) collective-permute-start(bf16[256,256]{1,0:T(8,128)(2,1)} %refs_0_.1), channel_id=1, source_target_pairs={{0,192},{64,0},{128,64},{192,128},{1,193},{65,1},{129,65},{193,129... | collective-permute-start | bytes 393224 | tf_op jit(solution)/shard_map/ppermute | solution.py:292
  17.6 6.0 %collective-permute-start.2 = (bf16[256,256]{1,0:T(8,128)(2,1)}, bf16[256,256]{1,0:T(8,128)(2,1)S(1)}, u32[]{:S(2)}, u32[]{:S(2)}) collective-permute-start(bf16[256,256]{1,0:T(8,128)(2,1)} %refs_0_.1), channel_id=1, source_target_pairs={{0,64},{64,128},{128,192},{192,0},{1,65},{65,129},{129,193},{193,1... | collective-permute-start | bytes 393224 | tf_op jit(solution)/shard_map/ppermute | solution.py:292
  18.2 7.7 %collective-permute-start.8 = (bf16[256,256]{1,0:T(8,128)(2,1)S(1)}, bf16[256,256]{1,0:T(8,128)(2,1)S(1)}, u32[]{:S(2)}, u32[]{:S(2)}) collective-permute-start(bf16[256,256]{1,0:T(8,128)(2,1)S(1)} %collective-permute-done.5.refs_4_), channel_id=1, source_target_pairs={{0,128},{64,192},{128,0},{192,64},{1,129},{65,193},{129,1},{193,65... | collective-permute-start | bytes 393224 | tf_op jit(solution)/shard_map/ppermute | solution.py:292
  20.8 7.0 %collective-permute-start.7 = (bf16[256,256]{1,0:T(8,128)(2,1)S(1)}, bf16[256,256]{1,0:T(8,128)(2,1)S(1)}, u32[]{:S(2)}, u32[]{:S(2)}) collective-permute-start(bf16[256,256]{1,0:T(8,128)(2,1)S(1)} %collective-permute-done.5.refs_4_), channel_id=1, source_target_pairs={{0,192},{64,0},{128,64},{192,128},{1,193},{65,1},{129,65},{193,129... | collective-permute-start | bytes 393224 | tf_op jit(solution)/shard_map/ppermute | solution.py:292
  21.7 7.9 %collective-permute-start.6 = (bf16[256,256]{1,0:T(8,128)(2,1)S(1)}, bf16[256,256]{1,0:T(8,128)(2,1)S(1)}, u32[]{:S(2)}, u32[]{:S(2)}) collective-permute-start(bf16[256,256]{1,0:T(8,128)(2,1)S(1)} %collective-permute-done.5.refs_4_), channel_id=1, source_target_pairs={{0,64},{64,128},{128,192},{192,0},{1,65},{65,129},{129,193},{193,1... | collective-permute-start | bytes 393224 | tf_op jit(solution)/shard_map/ppermute | solution.py:292
  22.3 14.9 %collective-permute-start = (bf16[512,256]{1,0:T(8,128)(2,1)S(1)}, bf16[512,256]{1,0:T(8,128)(2,1)S(1)}, u32[]{:S(2)}, u32[]{:S(2)}) collective-permute-start(bf16[512,256]{1,0:T(8,128)(2,1)S(1)} %bitcast.6), channel_id=1, source_target_pairs={{0,1},{1,0},{2,3},{3,2},{4,5},{5,4},{6,7},{7,6},{8,9},{9,8},{10,11... | collective-permute-start | bytes 786440 | tf_op jit(solution)/shard_map/ppermute | solution.py:304
  29.6 0.9 %copy-start = (bf16[256,256]{1,0:T(8,128)(2,1)S(1)}, bf16[256,256]{1,0:T(8,128)(2,1)}, u32[]{:S(2)}) copy-start(bf16[256,256]{1,0:T(8,128)(2,1)} %refs_0_.1) | copy-start | bytes 393220
  30.5 0.7 copy-start.3
  31.8 3.9 %collective-permute-start.9 = (bf16[2048,256]{1,0:T(8,128)(2,1)S(1)}, bf16[2048,256]{1,0:T(8,128)(2,1)S(1)}, u32[]{:S(2)}, u32[]{:S(2)}) collective-permute-start(bf16[2048,256]{1,0:T(8,128)(2,1)S(1)} %get-tuple-element.10.t_ref.ta_ref), channel_id=1, source_target_pairs={{0,32},{32,0},{1,33},{33,1},{2,34},{34,2},{3,35},{35,3},{4,36},{36... | collective-permute-start | bytes 3145736 | tf_op jit(solution)/shard_map/ppermute | solution.py:303
  37.1 10.4 %copy-start.1 = (f32[2048]{0:T(1024)S(1)}, f32[2048]{0:T(1024)}, u32[]{:S(2)}) copy-start(f32[2048]{0:T(1024)} %param.7) | copy-start | bytes 24580
  40.6 14.8 %all-to-all-start.1 = ((f32[16,8,128]{2,1,0:T(8,128)}), f32[16,8,128]{2,1,0:T(8,128)S(1)}, u32[]{:S(2)}, u32[]{:S(2)}) async-start(f32[16,8,128]{2,1,0:T(8,128)} %get-tuple-element.12), calls=%async_computation.1 | async-start | bytes 131072 | tf_op jit(solution)/shard_map/all_to_all | solution.py:337
  49.9 30.6 %copy-start.2 = (f32[2048]{0:T(1024)S(1)}, f32[2048]{0:T(1024)}, u32[]{:S(2)}) copy-start(f32[2048]{0:T(1024)} %param.8) | copy-start | bytes 24580

commit v3 on v2

--- a/solution.py
+++ b/solution.py
@@ -90,7 +90,7 @@
     return jnp.where(n == 2, 3, jnp.where(n == 3, 2, n))
 
 
-def join_kernel(scale, own_ref, pair_ref, gate_ref, *refs):
+def join_kernel(scale, gate_ref, own_ref, pair_ref, *refs):
     del gate_ref
     *pieces, near_ref, bias_ref = refs
     at = 0
@@ -98,15 +98,20 @@
         near_ref[at : at + piece.shape[0], :] = piece[...]
         at += piece.shape[0]
     x, c = lax.axis_index("x"), lax.axis_index("c")
-    row = 0
-    for other in range(NC):
-        for ref in (own_ref, pair_ref):
+
+    def put(ref, side):
+        row = 0
+        for other in range(NC):
             for k in SHIFTS:
                 block = lax.rem(x - k + NX, NX) * NC + lax.rem(c + other, NC)
                 for half in range(2):
                     values = ref[pl.ds(block * 2 + half, 1), :] * (1.0 / scale)
-                    bias_ref[row * LANES : (row + 1) * LANES, :] = spread(values)
-                    row += 1
+                    at = (row + 2 * side + half) * LANES
+                    bias_ref[at : at + LANES, :] = spread(values)
+                row += 4
+
+    put(own_ref, 0)
+    put(pair_ref, 1)
 
 
 def products(s_ref, t_ref, bufs):
@@ -223,8 +228,8 @@
     def put(strip, values):
         core = lax.rem(c + strip // count, NC)
         at = lax.rem(strip, count)
-        block = lax.rem(x - shift_of(lax.rem(at, NX)) + NX, NX) * NC + core
-        side = jnp.where(at < NX, mine, 1 - mine)
+        block = lax.rem(x - shift_of(at // 2) + NX, NX) * NC + core
+        side = jnp.where(lax.rem(at, 2) == 0, mine, 1 - mine)
         for h, value in enumerate(values):
             cols[side, pl.ds(block * 2 + h, 1), :] = value
 
@@ -289,17 +294,21 @@
     copies = jnp.broadcast_to(source_points[None], (NZ,) + source_points.shape)
     pair_points = lax.ppermute(target_points, "y", across)
     pair_potential = lax.ppermute(potential, "y", across)
-    pieces = [lax.ppermute(points, "x", around(NX, k)) if k else points for points in (target_points, pair_points) for k in SHIFTS]
+    own_potential = lax.ppermute(potential, "c", around(NC, 1))
+    mine = jnp.concatenate([target_points, pair_points], axis=0)
+    opposite = lax.ppermute(target_points, "x", around(NX, SHIFTS[-1]))
+    pieces = [mine] + [lax.ppermute(mine, "x", around(NX, k)) for k in SHIFTS[1:-1]]
+    pieces += [opposite, lax.ppermute(opposite, "y", across)]
     own = lax.all_to_all(copies, "z", 0, 0).reshape(-1, width)
-    block = len(pieces) * target_points.shape[0]
+    block = NX * mine.shape[0]
     near, bias = pl.pallas_call(
         functools.partial(join_kernel, scale),
         out_shape=[jax.ShapeDtypeStruct((block, width), jnp.bfloat16), jax.ShapeDtypeStruct((2 * block, LANES), f32)],
-        in_specs=[VMEM, VMEM, pl.BlockSpec(memory_space=pl.ANY)] + [VMEM] * len(pieces),
+        in_specs=[pl.BlockSpec(memory_space=pl.ANY)] + [VMEM] * (2 + len(pieces)),
         out_specs=[VMEM] * 2,
         compiler_params=params(16),
         cost_estimate=cost(8),
-    )(potential, pair_potential, own, *pieces)
+    )(own, own_potential, pair_potential, *pieces)
     far = lax.ppermute(near, "c", around(NC, 1))
     pair = lax.ppermute(own, "y", beside)
     chunk = own.shape[0]
@@ -314,7 +323,7 @@
         out_specs=VMEM,
         scratch_shapes=[buf] * 2,
         compiler_params=params(16),
-        cost_estimate=cost(1, 4e10),
+        cost_estimate=cost(1, 3e10),
     )(own, near, bias)
     second = pl.pallas_call(
         functools.partial(row_second, rate),

time: 81.6 us -> 78.8 us (0.966)
  waiting for transfers between devices: 14.9 us -> 8.78 us
  starting transfers between devices: 27.6 us -> 30.7 us
    ppermute x6 -> x5, waiting for transfers between devices: 6.83 us -> 0.01 us  [the longest x2 0.01 us: per_device(): lax.ppermute(mine, 'x', around(NX, k))]
    ppermute x1, starting transfers between devices: 0.1 us -> 2.57 us  [per_device(): pair_potential = lax.ppermute(potential, 'y', across)]
    all_to_all x1, waiting for transfers between devices: 0.01 us -> 2.23 us  [per_device(): own = lax.all_to_all(copies, 'z', 0, 0).reshape(-1, width)]
    ppermute x1, waiting for transfers between devices: 1.65 us -> 0.1 us  [per_device(): pair_potential = lax.ppermute(potential, 'y', across)]
    ppermute x1, starting transfers between devices: 1.65 us -> 2.91 us  [per_device(): far = lax.ppermute(near, 'c', around(NC, 1))]
    ppermute x1, starting transfers between devices: 2.73 us -> 3.65 us  [per_device(): pair_points = lax.ppermute(target_points, 'y', across)]
    all_to_all x1, starting transfers between devices: 9.01 us -> 8.19 us  [per_device(): own = lax.all_to_all(copies, 'z', 0, 0).reshape(-1, width)]
    ppermute x6 -> x5, starting transfers between devices: 6.67 us -> 7.03 us  [the longest x1 2.74 us: per_device(): opposite = lax.ppermute(target_points, 'x', around(NX, SHIFTS[-1]))]
  transfers between devices with their start and end apart: 12 -> 11, of which waited for: 7 -> 4; matrix products, arithmetic and copies ran while one was open for 0% -> 3% of each run, Pallas kernels for 7% -> 7%
where the time goes in v3:
time: 78.8 us; the launch traced here: 78.5 us
  starting transfers between devices  30.7 us (39%)
  Pallas kernels  20.5 us (26%)
  blocking collectives  15.3 us (19%)
  waiting for transfers between devices  8.78 us (11%)
  local copies, waits for them, and re-layouts  2.42 us (3%)
    all_to_all x1, blocking collectives, per_device(): lax.all_to_all(sent, ('x', 'c', 'y'), 0, 0, axis_index_groups=xc_across)  15.3 us
    pallas_call x1, Pallas kernels, per_device(): pl.pallas_call(functools.partial(col_kernel, rate), out_shape=jax.ShapeDt...  10.6 us
    all_to_all x1, starting transfers between devices, per_device(): own = lax.all_to_all(copies, 'z', 0, 0).reshape(-1, width)  8.19 us
    all_to_all x1, starting transfers between devices, per_device(): got = lax.all_to_all(sent, ('z', 'y'), 0, 0, axis_index_groups=z_beside)  6.37 us
    all_to_all x1, waiting for transfers between devices, per_device(): got = lax.all_to_all(sent, ('z', 'y'), 0, 0, axis_index_groups=z_beside)  5.51 us
    ppermute x1, starting transfers between devices, per_device(): pair_points = lax.ppermute(target_points, 'y', across)  3.65 us
    pallas_call x1, Pallas kernels, per_device(): pl.pallas_call(functools.partial(row_third, rate), out_shape=[jax.ShapeDt...  3.43 us
    ppermute x1, starting transfers between devices, per_device(): far = lax.ppermute(near, 'c', around(NC, 1))  2.91 us
  transfers between devices with their start and end apart: 11, of which 4 were waited for; matrix products, arithmetic and copies ran while one was open for 3% of the time, Pallas kernels for 7%

profile of v3, /device:TPU:1, one launch (start us, length us, event | category | flops | bytes accessed | tf_op | source)
XLA Modules:
  0.0 78.5 jit_solution(3141427595863054304)
XLA Ops:
  0.6 3.7 %collective-permute-start.3 = (bf16[256,256]{1,0:T(8,128)(2,1)}, bf16[256,256]{1,0:T(8,128)(2,1)S(1)}, u32[]{:S(2)}, u32[]{:S(2)}) collective-permute-start(bf16[256,256]{1,0:T(8,128)(2,1)} %param.6), channel_id=1, source_target_pairs={{0,3},{1,2},{2,1},{3,0},{4,7},{5,6},{6,5},{7,4},{8,11},{9,10},{10,... | collective-permute-start | bytes 393224 | tf_op jit(solution)/shard_map/ppermute | solution.py:295
  4.3 2.7 %collective-permute-start.6 = (bf16[256,256]{1,0:T(8,128)(2,1)}, bf16[256,256]{1,0:T(8,128)(2,1)S(1)}, u32[]{:S(2)}, u32[]{:S(2)}) collective-permute-start(bf16[256,256]{1,0:T(8,128)(2,1)} %param.6), channel_id=1, source_target_pairs={{0,128},{64,192},{128,0},{192,64},{1,129},{65,193},{129,1},{193,65... | collective-permute-start | bytes 393224 | tf_op jit(solution)/shard_map/ppermute | solution.py:299
  7.0 1.5 %broadcast_in_dim.2 = bf16[8,64,256]{2,1,0:T(8,128)(2,1)} broadcast(bf16[64,256]{1,0:T(8,128)(2,1)} %param.5), dimensions={1,2} | broadcast | bytes 294912 | tf_op jit(solution)/shard_map/broadcast_in_dim | solution.py:294
  8.5 8.2 %all-to-all-start = ((bf16[8,64,256]{2,1,0:T(8,128)(2,1)}), bf16[8,64,256]{2,1,0:T(8,128)(2,1)S(1)}, u32[]{:S(2)}, u32[]{:S(2)}) async-start(bf16[8,64,256]{2,1,0:T(8,128)(2,1)} %broadcast_in_dim.2), calls=%async_computation | async-start | bytes 524288 | tf_op jit(solution)/shard_map/all_to_all | solution.py:302
  16.7 0.9 %constant_dynamic-update-slice_fusion.1 = bf16[512,256]{1,0:T(8,128)(2,1)S(1)} fusion(bf16[256,256]{1,0:T(8,128)(2,1)} %param.6), kind=kLoop, calls=%fused_computation.1 | loop fusion | bytes 262144
  17.6 0.9 %collective-permute-start.5 = (bf16[512,256]{1,0:T(8,128)(2,1)S(1)}, bf16[512,256]{1,0:T(8,128)(2,1)S(1)}, u32[]{:S(2)}, u32[]{:S(2)}) collective-permute-start(bf16[512,256]{1,0:T(8,128)(2,1)S(1)} %constant_dynamic-update-slice_fusion.refs_0_), channel_id=1, source_target_pairs={{0,192},{64,0},{128,64},{192,128},{1,193},{65,1},{129,65},{193,129... | collective-permute-start | bytes 786440 | tf_op jit(solution)/shard_map/ppermute | solution.py:300
  18.6 0.6 collective-permute-start.4
  19.2 0.0 collective-permute-done.6.refs_3_
  19.2 0.1 collective-permute-start.7
  19.3 2.6 %collective-permute-start.2 = (f32[16,128]{1,0:T(8,128)}, f32[16,128]{1,0:T(8,128)S(1)}, u32[]{:S(2)}, u32[]{:S(2)}) collective-permute-start(f32[16,128]{1,0:T(8,128)} %bitcast.14), channel_id=1, source_target_pairs={{0,3},{1,2},{2,1},{3,0},{4,7},{5,6},{6,5},{7,4},{8,11},{9,10},{10,... | collective-permute-start | bytes 24584 | tf_op jit(solution)/shard_map/ppermute | solution.py:296
  21.9 2.6 %collective-permute-start.1 = (f32[16,128]{1,0:T(8,128)}, f32[16,128]{1,0:T(8,128)S(1)}, u32[]{:S(2)}, u32[]{:S(2)}) collective-permute-start(f32[16,128]{1,0:T(8,128)} %bitcast.15), channel_id=1, source_target_pairs={{0,32},{32,0},{1,33},{33,1},{2,34},{34,2},{3,35},{35,3},{4,36},{36... | collective-permute-start | bytes 24584 | tf_op jit(solution)/shard_map/ppermute | solution.py:297
  24.5 0.1 collective-permute-done.2.pair_ref
  24.6 2.2 %all-to-all-done = bf16[8,64,256]{2,1,0:T(8,128)(2,1)S(1)} async-done(((bf16[8,64,256]{2,1,0:T(8,128)(2,1)}), bf16[8,64,256]{2,1,0:T(8,128)(2,1)S(1)}, u32[]{:S(2)}, u32[]{:S(2)}) %all-to-all-start) | async-done | bytes 262176 | tf_op jit(solution)/shard_map/all_to_all | solution.py:302
  26.8 0.0 collective-permute-start
  26.8 0.0 collective-permute-done.1.own_ref
  26.8 0.0 collective-permute-done.7.refs_4_
  26.8 0.0 collective-permute-done.5.refs_2_
  26.8 0.0 collective-permute-done.4.refs_1_
  26.9 0.6 shard_map.68
  27.5 2.9 %collective-permute-start.8 = (bf16[2048,256]{1,0:T(8,128)(2,1)S(1)}, bf16[2048,256]{1,0:T(8,128)(2,1)S(1)}, u32[]{:S(2)}, u32[]{:S(2)}) collective-permute-start(bf16[2048,256]{1,0:T(8,128)(2,1)S(1)} %get-tuple-element.10.t_ref.ta_ref), channel_id=1, source_target_pairs={{0,32},{32,0},{1,33},{33,1},{2,34},{34,2},{3,35},{35,3},{4,36},{36... | collective-permute-start | bytes 3145736 | tf_op jit(solution)/shard_map/ppermute | solution.py:312
  30.4 1.4 %shard_map.69.first_ref = f32[4,128]{1,0:T(4,128)S(1)} custom-call(bf16[512,256]{1,0:T(8,128)(2,1)S(1)} %bitcast.8, bf16[2048,256]{1,0:T(8,128)(2,1)S(1)} %get-tuple-element.10.t_ref.ta_ref, f32[4096,128]{1,0:T(8,128)S(1)} %get-tuple-element.11.bias_ref), custom_call_target="tpu_custom_call" | custom-call | flops 30000001024 | bytes 1048576 | tf_op jit(solution)/shard_map/pallas_call | solution.py:319
  31.8 0.9 %collective-permute-done.8.t_ref.tb_ref = bf16[2048,256]{1,0:T(8,128)(2,1)S(1)} collective-permute-done((bf16[2048,256]{1,0:T(8,128)(2,1)S(1)}, bf16[2048,256]{1,0:T(8,128)(2,1)S(1)}, u32[]{:S(2)}, u32[]{:S(2)}) %collective-permute-start.8) | collective-permute-done | bytes 1048608 | tf_op jit(solution)/shard_map/ppermute | solution.py:312
  32.7 1.4 %shard_map.70.own_ref = f32[4,128]{1,0:T(4,128)S(1)} custom-call(bf16[512,256]{1,0:T(8,128)(2,1)S(1)} %bitcast.9, bf16[2048,256]{1,0:T(8,128)(2,1)S(1)} %collective-permute-done.8.t_ref.tb_ref, f32[4096,128]{1,0:T(8,128)S(1)} %get-tuple-element.11.bias_ref, f32[4,128]{1,0:T(4,128)S(1)} %shard_map.69.first_ref), custom_call_target="tpu_custom_call" | custom-call | bytes 262144 | tf_op jit(solution)/shard_map/pallas_call | solution.py:328
  34.1 0.0 copy-start
  34.1 3.4 %shard_map.71 = (f32[16,8,128]{2,1,0:T(8,128)}, f32[8,128]{1,0:T(8,128)S(1)}) custom-call(bf16[512,256]{1,0:T(8,128)(2,1)S(1)} %collective-permute-done.s_ref.s1, bf16[2048,256]{1,0:T(8,128)(2,1)S(1)} %get-tuple-element.10.t_ref.ta_ref, bf16[2048,256]{1,0:T(8,128)(2,1)S(1)} %collective-permute-done.8.t_ref.tb_ref, ...), custom_call_target="tpu_custom_call" | custom-call | bytes 16777216 | tf_op jit(solution)/shard_map/pallas_call | solution.py:337
  37.5 6.4 %all-to-all-start.1 = ((f32[16,8,128]{2,1,0:T(8,128)}), f32[16,8,128]{2,1,0:T(8,128)S(1)}, u32[]{:S(2)}, u32[]{:S(2)}) async-start(f32[16,8,128]{2,1,0:T(8,128)} %get-tuple-element.12), calls=%async_computation.1 | async-start | bytes 131072 | tf_op jit(solution)/shard_map/all_to_all | solution.py:346
  43.9 2.4 %shard_map.72 = (f32[32,128]{1,0:T(8,128)S(1)}, f32[8,128]{1,0:T(8,128)S(1)}) custom-call(f32[8,128]{1,0:T(8,128)S(1)} %get-tuple-element.13.rows_ref, f32[16,128]{1,0:T(8,128)S(1)} %bitcast.12, bf16[512,256]{1,0:T(8,128)(2,1)S(1)} %bitcast.10, bf16[512,256]{1,0:T(8,128)(2,1)S(1)} %collective-permute-done.s_ref.s1, ...), custom_call_target="tpu_custom_call" | custom-call | bytes 16777216 | tf_op jit(solution)/shard_map/pallas_call | solution.py:350
  46.3 0.0 copy-start.1
  46.3 5.5 %all-to-all-done.1.got_ref = f32[16,8,128]{2,1,0:T(8,128)S(1)} async-done(((f32[16,8,128]{2,1,0:T(8,128)}), f32[16,8,128]{2,1,0:T(8,128)S(1)}, u32[]{:S(2)}, u32[]{:S(2)}) %all-to-all-start.1) | async-done | bytes 65568 | tf_op jit(solution)/shard_map/all_to_all | solution.py:346
  51.8 10.6 %shard_map.73 = f32[16,24,128]{2,1,0:T(8,128)S(1)} custom-call(f32[16,8,128]{2,1,0:T(8,128)S(1)} %all-to-all-done.1.got_ref, f32[8,128]{1,0:T(8,128)S(1)} %get-tuple-element.13.rows_ref, f32[8,128]{1,0:T(8,128)S(1)} %get-tuple-element.14.ready_ref, f32[32,128]{1,0:T(8,128)S(1)} %get-tuple-element.15.top_ref, bf16[512,256]{1,0:T(8,128)(2,1)S(1)} %bitcast.11, ...), custom_call_target="tpu_custom_call" | custom-call | bytes 16777216 | tf_op jit(solution)/shard_map/pallas_call | solution.py:359
  62.5 15.3 %all_to_all.15.got_ref = f32[16,24,128]{2,1,0:T(8,128)S(1)} all-to-all(f32[16,24,128]{2,1,0:T(8,128)S(1)} %shard_map.73), channel_id=1, replica_groups={{0,3,32,35,64,67,96,99,128,131,160,163,192,195,224,227},{1,2,33,34,65,6..., dimensions={0} | all-to-all | bytes 393216 | tf_op jit(solution)/shard_map/all_to_all | solution.py:368
  77.8 0.7 shard_map.74
  (5 shorter events, 0.0 us)
Async XLA Ops:
  0.6 17.0 %collective-permute-start.3 = (bf16[256,256]{1,0:T(8,128)(2,1)}, bf16[256,256]{1,0:T(8,128)(2,1)S(1)}, u32[]{:S(2)}, u32[]{:S(2)}) collective-permute-start(bf16[256,256]{1,0:T(8,128)(2,1)} %param.6), channel_id=1, source_target_pairs={{0,3},{1,2},{2,1},{3,0},{4,7},{5,6},{6,5},{7,4},{8,11},{9,10},{10,... | collective-permute-start | bytes 393224 | tf_op jit(solution)/shard_map/ppermute | solution.py:295
  4.3 14.9 %collective-permute-start.6 = (bf16[256,256]{1,0:T(8,128)(2,1)}, bf16[256,256]{1,0:T(8,128)(2,1)S(1)}, u32[]{:S(2)}, u32[]{:S(2)}) collective-permute-start(bf16[256,256]{1,0:T(8,128)(2,1)} %param.6), channel_id=1, source_target_pairs={{0,128},{64,192},{128,0},{192,64},{1,129},{65,193},{129,1},{193,65... | collective-permute-start | bytes 393224 | tf_op jit(solution)/shard_map/ppermute | solution.py:299
  8.5 18.3 %all-to-all-start = ((bf16[8,64,256]{2,1,0:T(8,128)(2,1)}), bf16[8,64,256]{2,1,0:T(8,128)(2,1)S(1)}, u32[]{:S(2)}, u32[]{:S(2)}) async-start(bf16[8,64,256]{2,1,0:T(8,128)(2,1)} %broadcast_in_dim.2), calls=%async_computation | async-start | bytes 524288 | tf_op jit(solution)/shard_map/all_to_all | solution.py:302
  17.6 9.2 %collective-permute-start.5 = (bf16[512,256]{1,0:T(8,128)(2,1)S(1)}, bf16[512,256]{1,0:T(8,128)(2,1)S(1)}, u32[]{:S(2)}, u32[]{:S(2)}) collective-permute-start(bf16[512,256]{1,0:T(8,128)(2,1)S(1)} %constant_dynamic-update-slice_fusion.refs_0_), channel_id=1, source_target_pairs={{0,192},{64,0},{128,64},{192,128},{1,193},{65,1},{129,65},{193,129... | collective-permute-start | bytes 786440 | tf_op jit(solution)/shard_map/ppermute | solution.py:300
  18.6 8.3 %collective-permute-start.4 = (bf16[512,256]{1,0:T(8,128)(2,1)S(1)}, bf16[512,256]{1,0:T(8,128)(2,1)S(1)}, u32[]{:S(2)}, u32[]{:S(2)}) collective-permute-start(bf16[512,256]{1,0:T(8,128)(2,1)S(1)} %constant_dynamic-update-slice_fusion.refs_0_), channel_id=1, source_target_pairs={{0,64},{64,128},{128,192},{192,0},{1,65},{65,129},{129,193},{193,1... | collective-permute-start | bytes 786440 | tf_op jit(solution)/shard_map/ppermute | solution.py:300
  19.2 7.7 %collective-permute-start.7 = (bf16[256,256]{1,0:T(8,128)(2,1)S(1)}, bf16[256,256]{1,0:T(8,128)(2,1)S(1)}, u32[]{:S(2)}, u32[]{:S(2)}) collective-permute-start(bf16[256,256]{1,0:T(8,128)(2,1)S(1)} %collective-permute-done.6.refs_3_), channel_id=1, source_target_pairs={{0,3},{1,2},{2,1},{3,0},{4,7},{5,6},{6,5},{7,4},{8,11},{9,10},{10,... | collective-permute-start | bytes 393224 | tf_op jit(solution)/shard_map/ppermute | solution.py:301
  19.3 5.3 %collective-permute-start.2 = (f32[16,128]{1,0:T(8,128)}, f32[16,128]{1,0:T(8,128)S(1)}, u32[]{:S(2)}, u32[]{:S(2)}) collective-permute-start(f32[16,128]{1,0:T(8,128)} %bitcast.14), channel_id=1, source_target_pairs={{0,3},{1,2},{2,1},{3,0},{4,7},{5,6},{6,5},{7,4},{8,11},{9,10},{10,... | collective-permute-start | bytes 24584 | tf_op jit(solution)/shard_map/ppermute | solution.py:296
  21.9 5.0 %collective-permute-start.1 = (f32[16,128]{1,0:T(8,128)}, f32[16,128]{1,0:T(8,128)S(1)}, u32[]{:S(2)}, u32[]{:S(2)}) collective-permute-start(f32[16,128]{1,0:T(8,128)} %bitcast.15), channel_id=1, source_target_pairs={{0,32},{32,0},{1,33},{33,1},{2,34},{34,2},{3,35},{35,3},{4,36},{36... | collective-permute-start | bytes 24584 | tf_op jit(solution)/shard_map/ppermute | solution.py:297
  26.8 7.2 %collective-permute-start = (bf16[512,256]{1,0:T(8,128)(2,1)S(1)}, bf16[512,256]{1,0:T(8,128)(2,1)S(1)}, u32[]{:S(2)}, u32[]{:S(2)}) collective-permute-start(bf16[512,256]{1,0:T(8,128)(2,1)S(1)} %bitcast.6), channel_id=1, source_target_pairs={{0,1},{1,0},{2,3},{3,2},{4,5},{5,4},{6,7},{7,6},{8,9},{9,8},{10,11... | collective-permute-start | bytes 786440 | tf_op jit(solution)/shard_map/ppermute | solution.py:313
  27.5 5.2 %collective-permute-start.8 = (bf16[2048,256]{1,0:T(8,128)(2,1)S(1)}, bf16[2048,256]{1,0:T(8,128)(2,1)S(1)}, u32[]{:S(2)}, u32[]{:S(2)}) collective-permute-start(bf16[2048,256]{1,0:T(8,128)(2,1)S(1)} %get-tuple-element.10.t_ref.ta_ref), channel_id=1, source_target_pairs={{0,32},{32,0},{1,33},{33,1},{2,34},{34,2},{3,35},{35,3},{4,36},{36... | collective-permute-start | bytes 3145736 | tf_op jit(solution)/shard_map/ppermute | solution.py:312
  34.1 9.8 %copy-start = (f32[2048]{0:T(1024)S(1)}, f32[2048]{0:T(1024)}, u32[]{:S(2)}) copy-start(f32[2048]{0:T(1024)} %param.7) | copy-start | bytes 24580
  37.5 14.3 %all-to-all-start.1 = ((f32[16,8,128]{2,1,0:T(8,128)}), f32[16,8,128]{2,1,0:T(8,128)S(1)}, u32[]{:S(2)}, u32[]{:S(2)}) async-start(f32[16,8,128]{2,1,0:T(8,128)} %get-tuple-element.12), calls=%async_computation.1 | async-start | bytes 131072 | tf_op jit(solution)/shard_map/all_to_all | solution.py:346
  46.3 31.5 %copy-start.1 = (f32[2048]{0:T(1024)S(1)}, f32[2048]{0:T(1024)}, u32[]{:S(2)}) copy-start(f32[2048]{0:T(1024)} %param.8) | copy-start | bytes 24580

commit v4 on v3

--- a/solution.py
+++ b/solution.py
@@ -90,55 +90,59 @@
     return jnp.where(n == 2, 3, jnp.where(n == 3, 2, n))
 
 
+def pack_kernel(targets_ref, tp_ref, packed_ref, own_ref):
+    rows = targets_ref.shape[0]
+    packed_ref[:rows, :] = targets_ref[...]
+    own_ref[...] = tp_ref[...]
+    blocks = tp_ref.shape[0] // 2
+    rest = jnp.concatenate([tp_ref[pl.ds(half, blocks, stride=2), :] for half in range(2)], axis=1)
+    parts = []
+    for _ in range(3):
+        parts.append(rest.astype(jnp.bfloat16).astype(f32))
+        rest = rest - parts[-1]
+    parts.append(jnp.zeros_like(rest))
+    packed_ref[rows:, :] = jnp.concatenate(parts, axis=0).astype(jnp.bfloat16)
+
+
 def join_kernel(scale, gate_ref, own_ref, pair_ref, *refs):
     del gate_ref
-    *pieces, near_ref, bias_ref = refs
+    *pieces, near_ref, bias_ref, sums_ref = refs
     at = 0
     for piece in pieces:
         near_ref[at : at + piece.shape[0], :] = piece[...]
         at += piece.shape[0]
+    near_ref[at:, :] = pair_ref[: near_ref.shape[0] - at, :]
+    blocks = sums_ref.shape[0] // 2
+    parts = pair_ref[pair_ref.shape[0] - 4 * blocks :, :].astype(f32)
+    sums = parts[:blocks] + (parts[blocks : 2 * blocks] + parts[2 * blocks : 3 * blocks])
+    for half, lanes in halves():
+        sums_ref[half * blocks : (half + 1) * blocks, :] = sums[:, lanes]
     x, c = lax.axis_index("x"), lax.axis_index("c")
-
-    def put(ref, side):
-        row = 0
-        for other in range(NC):
-            for k in SHIFTS:
-                block = lax.rem(x - k + NX, NX) * NC + lax.rem(c + other, NC)
-                for half in range(2):
-                    values = ref[pl.ds(block * 2 + half, 1), :] * (1.0 / scale)
-                    at = (row + 2 * side + half) * LANES
-                    bias_ref[at : at + LANES, :] = spread(values)
-                row += 4
-
-    put(own_ref, 0)
-    put(pair_ref, 1)
-
-
-def products(s_ref, t_ref, bufs):
+    row = 0
+    for other in range(NC):
+        for k in SHIFTS:
+            block = lax.rem(x - k + NX, NX) * NC + lax.rem(c + other, NC)
+            values = [own_ref[pl.ds(block * 2 + half, 1), :] for half in range(2)]
+            values += [sums_ref[pl.ds(half * blocks + block, 1), :] for half in range(2)]
+            for value in values:
+                bias_ref[row * LANES : (row + 1) * LANES, :] = spread(value * (1.0 / scale))
+                row += 1
+
+
+def row_part(rate, s_ref, t_ref, bias_ref, base, bufs):
     for n, buf in enumerate(bufs):
         buf[...] = contract(t_ref[...], s_ref[n * STRIP : (n + 1) * STRIP, :])
-
-
-def row_first(rate, s_ref, t_ref, bias_ref, out_ref, buf0, buf1):
-    products(s_ref, t_ref, (buf0, buf1))
-    out_ref[...] = jnp.concatenate(lse_of(buf0, bias_ref, rate) + lse_of(buf1, bias_ref, rate), axis=0)
-
-
-def row_second(rate, s_ref, t_ref, bias_ref, first_ref, out_ref, buf0, buf1):
-    products(s_ref, t_ref, (buf0, buf1))
+    return jnp.concatenate([row for buf in bufs for row in lse_of(buf, bias_ref, rate, base)], axis=0)
+
+
+def row_near(rate, s_ref, t_ref, bias_ref, out_ref, buf0, buf1):
+    out_ref[...] = row_part(rate, s_ref, t_ref, bias_ref, 0, (buf0, buf1))
+
+
+def row_far(rate, own_ref, pair_ref, t_ref, bias_ref, own_near, pair_near, out_ref, rows_ref, buf0, buf1, buf2, buf3):
     base = t_ref.shape[0]
-    mine = jnp.concatenate(lse_of(buf0, bias_ref, rate, base) + lse_of(buf1, bias_ref, rate, base), axis=0)
-    out_ref[...] = lse_parts(jnp.stack([first_ref[...], mine]), rate)
-
-
-def row_third(rate, s_ref, ta_ref, tb_ref, bias_ref, own_ref, out_ref, rows_ref, buf0, buf1, buf2, buf3):
-    products(s_ref, ta_ref, (buf0, buf1))
-    products(s_ref, tb_ref, (buf2, buf3))
-    base = ta_ref.shape[0]
-    near = jnp.concatenate(lse_of(buf0, bias_ref, rate) + lse_of(buf1, bias_ref, rate), axis=0)
-    far = jnp.concatenate(lse_of(buf2, bias_ref, rate, base) + lse_of(buf3, bias_ref, rate, base), axis=0)
-    pair = lse_parts(jnp.stack([near, far]), rate)
-    own = own_ref[...]
+    own = lse_parts(jnp.stack([own_near[...], row_part(rate, own_ref, t_ref, bias_ref, base, (buf0, buf1))]), rate)
+    pair = lse_parts(jnp.stack([pair_near[...], row_part(rate, pair_ref, t_ref, bias_ref, base, (buf2, buf3))]), rate)
     low = lax.rem(lax.axis_index("y"), 2) == 0
     rows = jnp.concatenate([jnp.where(low, own, pair), jnp.where(low, pair, own)], axis=0)
     rows_ref[...] = rows
@@ -293,12 +297,21 @@
     potential = target_potential.reshape(-1, LANES)
     copies = jnp.broadcast_to(source_points[None], (NZ,) + source_points.shape)
     pair_points = lax.ppermute(target_points, "y", across)
-    pair_potential = lax.ppermute(potential, "y", across)
-    own_potential = lax.ppermute(potential, "c", around(NC, 1))
     mine = jnp.concatenate([target_points, pair_points], axis=0)
     opposite = lax.ppermute(target_points, "x", around(NX, SHIFTS[-1]))
-    pieces = [mine] + [lax.ppermute(mine, "x", around(NX, k)) for k in SHIFTS[1:-1]]
-    pieces += [opposite, lax.ppermute(opposite, "y", across)]
+    pieces = [mine] + [lax.ppermute(mine, "x", around(NX, k)) for k in SHIFTS[1:-1]] + [opposite]
+    packed, own_potential = pl.pallas_call(
+        pack_kernel,
+        out_shape=[
+            jax.ShapeDtypeStruct((opposite.shape[0] + 2 * potential.shape[0], width), jnp.bfloat16),
+            jax.ShapeDtypeStruct(potential.shape, f32),
+        ],
+        in_specs=[VMEM] * 2,
+        out_specs=[VMEM] * 2,
+        compiler_params=params(16),
+        cost_estimate=cost(0.001),
+    )(opposite, potential)
+    pair_packed = lax.ppermute(packed, "y", across)
     own = lax.all_to_all(copies, "z", 0, 0).reshape(-1, width)
     block = NX * mine.shape[0]
     near, bias = pl.pallas_call(
@@ -306,9 +319,10 @@
         out_shape=[jax.ShapeDtypeStruct((block, width), jnp.bfloat16), jax.ShapeDtypeStruct((2 * block, LANES), f32)],
         in_specs=[pl.BlockSpec(memory_space=pl.ANY)] + [VMEM] * (2 + len(pieces)),
         out_specs=[VMEM] * 2,
+        scratch_shapes=[pltpu.VMEM(potential.shape, f32)],
         compiler_params=params(16),
         cost_estimate=cost(8),
-    )(own, own_potential, pair_potential, *pieces)
+    )(own, own_potential, pair_packed, *pieces)
     far = lax.ppermute(near, "c", around(NC, 1))
     pair = lax.ppermute(own, "y", beside)
     chunk = own.shape[0]
@@ -316,33 +330,27 @@
 
     buf = pltpu.VMEM((block, STRIP), f32)
     part = jax.ShapeDtypeStruct((chunk // LANES, LANES), f32)
-    first = pl.pallas_call(
-        functools.partial(row_first, rate),
-        out_shape=part,
-        in_specs=[VMEM] * 3,
-        out_specs=VMEM,
-        scratch_shapes=[buf] * 2,
-        compiler_params=params(16),
-        cost_estimate=cost(1, 3e10),
-    )(own, near, bias)
-    second = pl.pallas_call(
-        functools.partial(row_second, rate),
-        out_shape=part,
-        in_specs=[VMEM] * 4,
-        out_specs=VMEM,
-        scratch_shapes=[buf] * 2,
-        compiler_params=params(16),
-        cost_estimate=cost(0.25),
-    )(own, far, bias, first)
+    def over_near(sources, weight):
+        return pl.pallas_call(
+            functools.partial(row_near, rate),
+            out_shape=part,
+            in_specs=[VMEM] * 3,
+            out_specs=VMEM,
+            scratch_shapes=[buf] * 2,
+            compiler_params=params(16),
+            cost_estimate=weight,
+        )(sources, near, bias)
+
+    own_near, pair_near = over_near(own, cost(1, 3e10)), over_near(pair, cost(0.25))
     sent, rows = pl.pallas_call(
-        functools.partial(row_third, rate),
+        functools.partial(row_far, rate),
         out_shape=[jax.ShapeDtypeStruct((2 * NZ, sub, LANES), f32), jax.ShapeDtypeStruct((sub, LANES), f32)],
-        in_specs=[VMEM] * 5,
+        in_specs=[VMEM] * 6,
         out_specs=[VMEM] * 2,
         scratch_shapes=[buf] * 4,
         compiler_params=params(16),
         cost_estimate=cost(16),
-    )(pair, near, far, bias, second)
+    )(own, pair, far, bias, own_near, pair_near)
     got = lax.all_to_all(sent, ("z", "y"), 0, 0, axis_index_groups=z_beside)
 
     strips = 2 * block // STRIP

time: 78.8 us -> 76 us (0.964)
  starting transfers between devices: 30.7 us -> 24.7 us
  waiting for transfers between devices: 8.78 us -> 12.5 us
  blocking collectives: 15.3 us -> 14 us
    ppermute x3 -> x1, starting transfers between devices: 5.31 us -> 0.19 us  [per_device(): pair_packed = lax.ppermute(packed, 'y', across)]
    all_to_all x1, waiting for transfers between devices: 2.23 us -> 6.74 us  [per_device(): own = lax.all_to_all(copies, 'z', 0, 0).reshape(-1, width)]
    all_to_all x1, blocking collectives: 15.3 us -> 14 us  [per_device(): lax.all_to_all(sent, ('x', 'c', 'y'), 0, 0, axis_index_groups=xc_across)]
    ppermute x1, waiting for transfers between devices: 0.92 us -> 0.01 us  [per_device(): far = lax.ppermute(near, 'c', around(NC, 1))]
    all_to_all x1, starting transfers between devices: 6.37 us -> 5.51 us  [per_device(): got = lax.all_to_all(sent, ('z', 'y'), 0, 0, axis_index_groups=z_beside)]
    unnamed x5 -> x7, local copies, waits for them, and re-layouts: 0.93 us -> 1.62 us
    pallas_call x3 -> x4, Pallas kernels: 6.16 us -> 6.14 us  [the longest x1 3.4 us: per_device(): pl.pallas_call(functools.partial(row_far, rate), out_shape=[jax.ShapeDtyp...]
  transfers between devices with their start and end apart: 11 -> 9, of which waited for: 4 -> 3; matrix products, arithmetic and copies ran while one was open for 3% -> 3% of each run, Pallas kernels for 7% -> 8%
where the time goes in v4:
time: 76 us; the launch traced here: 75.6 us
  starting transfers between devices  24.7 us (32%)
  Pallas kernels  20.5 us (27%)
  blocking collectives  14 us (18%)
  waiting for transfers between devices  12.5 us (16%)
  local copies, waits for them, and re-layouts  3.11 us (4%)
    all_to_all x1, blocking collectives, per_device(): lax.all_to_all(sent, ('x', 'c', 'y'), 0, 0, axis_index_groups=xc_across)  14 us
    pallas_call x1, Pallas kernels, per_device(): pl.pallas_call(functools.partial(col_kernel, rate), out_shape=jax.ShapeDt...  10.6 us
    all_to_all x1, starting transfers between devices, per_device(): own = lax.all_to_all(copies, 'z', 0, 0).reshape(-1, width)  8.19 us
    all_to_all x1, waiting for transfers between devices, per_device(): own = lax.all_to_all(copies, 'z', 0, 0).reshape(-1, width)  6.74 us
    all_to_all x1, starting transfers between devices, per_device(): got = lax.all_to_all(sent, ('z', 'y'), 0, 0, axis_index_groups=z_beside)  5.51 us
    all_to_all x1, waiting for transfers between devices, per_device(): got = lax.all_to_all(sent, ('z', 'y'), 0, 0, axis_index_groups=z_beside)  5.45 us
    ppermute x1, starting transfers between devices, per_device(): pair_points = lax.ppermute(target_points, 'y', across)  3.65 us
    pallas_call x1, Pallas kernels, per_device(): pl.pallas_call(functools.partial(row_far, rate), out_shape=[jax.ShapeDtyp...  3.4 us
  transfers between devices with their start and end apart: 9, of which 3 were waited for; matrix products, arithmetic and copies ran while one was open for 3% of the time, Pallas kernels for 8%

profile of v4, /device:TPU:1, one launch (start us, length us, event | category | flops | bytes accessed | tf_op | source)
XLA Modules:
  0.0 75.6 jit_solution(15229548547243594542)
XLA Ops:
  0.6 3.7 %collective-permute-start.3 = (bf16[256,256]{1,0:T(8,128)(2,1)}, bf16[256,256]{1,0:T(8,128)(2,1)S(1)}, u32[]{:S(2)}, u32[]{:S(2)}) collective-permute-start(bf16[256,256]{1,0:T(8,128)(2,1)} %param.6), channel_id=1, source_target_pairs={{0,3},{1,2},{2,1},{3,0},{4,7},{5,6},{6,5},{7,4},{8,11},{9,10},{10,... | collective-permute-start | bytes 393224 | tf_op jit(solution)/shard_map/ppermute | solution.py:299
  4.3 2.7 %collective-permute-start.1 = (bf16[256,256]{1,0:T(8,128)(2,1)}, bf16[256,256]{1,0:T(8,128)(2,1)S(1)}, u32[]{:S(2)}, u32[]{:S(2)}) collective-permute-start(bf16[256,256]{1,0:T(8,128)(2,1)} %param.6), channel_id=1, source_target_pairs={{0,128},{64,192},{128,0},{192,64},{1,129},{65,193},{129,1},{193,65... | collective-permute-start | bytes 393224 | tf_op jit(solution)/shard_map/ppermute | solution.py:301
  7.0 1.5 %broadcast_in_dim.2 = bf16[8,64,256]{2,1,0:T(8,128)(2,1)} broadcast(bf16[64,256]{1,0:T(8,128)(2,1)} %param.5), dimensions={1,2} | broadcast | bytes 294912 | tf_op jit(solution)/shard_map/broadcast_in_dim | solution.py:298
  8.5 8.2 %all-to-all-start = ((bf16[8,64,256]{2,1,0:T(8,128)(2,1)}), bf16[8,64,256]{2,1,0:T(8,128)(2,1)S(1)}, u32[]{:S(2)}, u32[]{:S(2)}) async-start(bf16[8,64,256]{2,1,0:T(8,128)(2,1)} %broadcast_in_dim.2), calls=%async_computation | async-start | bytes 524288 | tf_op jit(solution)/shard_map/all_to_all | solution.py:315
  16.7 0.9 %constant_dynamic-update-slice_fusion.1 = bf16[512,256]{1,0:T(8,128)(2,1)S(1)} fusion(bf16[256,256]{1,0:T(8,128)(2,1)} %param.6), kind=kLoop, calls=%fused_computation.1 | loop fusion | bytes 262144
  17.6 0.0 collective-permute-done.3
  17.6 0.9 %collective-permute-start.5 = (bf16[512,256]{1,0:T(8,128)(2,1)S(1)}, bf16[512,256]{1,0:T(8,128)(2,1)S(1)}, u32[]{:S(2)}, u32[]{:S(2)}) collective-permute-start(bf16[512,256]{1,0:T(8,128)(2,1)S(1)} %constant_dynamic-update-slice_fusion.refs_0_), channel_id=1, source_target_pairs={{0,192},{64,0},{128,64},{192,128},{1,193},{65,1},{129,65},{193,129... | collective-permute-start | bytes 786440 | tf_op jit(solution)/shard_map/ppermute | solution.py:302
  18.6 0.6 collective-permute-start.4
  19.2 0.0 collective-permute-done.1.targets_ref.refs_3_
  19.2 0.7 copy-done.1
  19.9 0.2 collective-permute-start.2
  20.1 6.7 %all-to-all-done = bf16[8,64,256]{2,1,0:T(8,128)(2,1)S(1)} async-done(((bf16[8,64,256]{2,1,0:T(8,128)(2,1)}), bf16[8,64,256]{2,1,0:T(8,128)(2,1)S(1)}, u32[]{:S(2)}, u32[]{:S(2)}) %all-to-all-start) | async-done | bytes 262176 | tf_op jit(solution)/shard_map/all_to_all | solution.py:315
  26.8 0.0 collective-permute-start
  26.8 0.0 collective-permute-done.2.pair_ref
  26.8 0.0 collective-permute-done.5.refs_2_
  26.8 0.0 collective-permute-done.4.refs_1_
  26.8 0.6 shard_map.69
  27.5 2.9 %collective-permute-start.6 = (bf16[2048,256]{1,0:T(8,128)(2,1)S(1)}, bf16[2048,256]{1,0:T(8,128)(2,1)S(1)}, u32[]{:S(2)}, u32[]{:S(2)}) collective-permute-start(bf16[2048,256]{1,0:T(8,128)(2,1)S(1)} %get-tuple-element.14.t_ref.ta_ref), channel_id=1, source_target_pairs={{0,32},{32,0},{1,33},{33,1},{2,34},{34,2},{3,35},{35,3},{4,36},{36... | collective-permute-start | bytes 3145736 | tf_op jit(solution)/shard_map/ppermute | solution.py:326
  30.4 1.4 %shard_map.70.own_near = f32[4,128]{1,0:T(4,128)S(1)} custom-call(bf16[512,256]{1,0:T(8,128)(2,1)S(1)} %bitcast.8, bf16[2048,256]{1,0:T(8,128)(2,1)S(1)} %get-tuple-element.14.t_ref.ta_ref, f32[4096,128]{1,0:T(8,128)S(1)} %get-tuple-element.15.bias_ref), custom_call_target="tpu_custom_call" | custom-call | flops 30000001024 | bytes 1048576 | tf_op jit(solution)/shard_map/pallas_call | solution.py:334
  31.8 0.3 collective-permute-done.s_ref.pair_ref.s1
  32.0 1.4 %shard_map.71.pair_near = f32[4,128]{1,0:T(4,128)S(1)} custom-call(bf16[512,256]{1,0:T(8,128)(2,1)S(1)} %collective-permute-done.s_ref.pair_ref.s1, bf16[2048,256]{1,0:T(8,128)(2,1)S(1)} %get-tuple-element.14.t_ref.ta_ref, f32[4096,128]{1,0:T(8,128)S(1)} %get-tuple-element.15.bias_ref), custom_call_target="tpu_custom_call" | custom-call | bytes 262144 | tf_op jit(solution)/shard_map/pallas_call | solution.py:334
  33.4 0.0 copy-start
  33.4 0.0 collective-permute-done.6.t_ref.tb_ref
  33.4 3.4 %shard_map.72 = (f32[16,8,128]{2,1,0:T(8,128)}, f32[8,128]{1,0:T(8,128)S(1)}) custom-call(bf16[512,256]{1,0:T(8,128)(2,1)S(1)} %bitcast.9, bf16[512,256]{1,0:T(8,128)(2,1)S(1)} %collective-permute-done.s_ref.pair_ref.s1, bf16[2048,256]{1,0:T(8,128)(2,1)S(1)} %collective-permute-done.6.t_ref.tb_ref, f32[4096,128]{1,0:T(8,128)S(1)} %get-tuple-element.15.bias_ref, ...), custom_call_target="tpu_custom_call" | custom-call | bytes 16777216 | tf_op jit(solution)/shard_map/pallas_call | solution.py:345
  36.8 5.5 %all-to-all-start.1 = ((f32[16,8,128]{2,1,0:T(8,128)}), f32[16,8,128]{2,1,0:T(8,128)S(1)}, u32[]{:S(2)}, u32[]{:S(2)}) async-start(f32[16,8,128]{2,1,0:T(8,128)} %get-tuple-element.16), calls=%async_computation.1 | async-start | bytes 131072 | tf_op jit(solution)/shard_map/all_to_all | solution.py:354
  42.3 0.0 copy-done
  42.4 2.4 %shard_map.73 = (f32[32,128]{1,0:T(8,128)S(1)}, f32[8,128]{1,0:T(8,128)S(1)}) custom-call(f32[8,128]{1,0:T(8,128)S(1)} %get-tuple-element.17.rows_ref, f32[16,128]{1,0:T(8,128)S(1)} %bitcast.12, bf16[512,256]{1,0:T(8,128)(2,1)S(1)} %bitcast.10, bf16[512,256]{1,0:T(8,128)(2,1)S(1)} %collective-permute-done.s_ref.pair_ref.s1, ...), custom_call_target="tpu_custom_call" | custom-call | bytes 16777216 | tf_op jit(solution)/shard_map/pallas_call | solution.py:358
  44.8 0.0 copy-start.2
  44.8 5.5 %all-to-all-done.1.got_ref = f32[16,8,128]{2,1,0:T(8,128)S(1)} async-done(((f32[16,8,128]{2,1,0:T(8,128)}), f32[16,8,128]{2,1,0:T(8,128)S(1)}, u32[]{:S(2)}, u32[]{:S(2)}) %all-to-all-start.1) | async-done | bytes 65568 | tf_op jit(solution)/shard_map/all_to_all | solution.py:354
  50.3 10.6 %shard_map.74 = f32[16,24,128]{2,1,0:T(8,128)S(1)} custom-call(f32[16,8,128]{2,1,0:T(8,128)S(1)} %all-to-all-done.1.got_ref, f32[8,128]{1,0:T(8,128)S(1)} %get-tuple-element.17.rows_ref, f32[8,128]{1,0:T(8,128)S(1)} %get-tuple-element.18.ready_ref, f32[32,128]{1,0:T(8,128)S(1)} %get-tuple-element.19.top_ref, bf16[512,256]{1,0:T(8,128)(2,1)S(1)} %bitcast.11, ...), custom_call_target="tpu_custom_call" | custom-call | bytes 16777216 | tf_op jit(solution)/shard_map/pallas_call | solution.py:367
  60.9 14.0 %all_to_all.15.got_ref = f32[16,24,128]{2,1,0:T(8,128)S(1)} all-to-all(f32[16,24,128]{2,1,0:T(8,128)S(1)} %shard_map.74), channel_id=1, replica_groups={{0,3,32,35,64,67,96,99,128,131,160,163,192,195,224,227},{1,2,33,34,65,6..., dimensions={0} | all-to-all | bytes 393216 | tf_op jit(solution)/shard_map/all_to_all | solution.py:376
  74.9 0.7 shard_map.75
  (4 shorter events, 0.0 us)
Async XLA Ops:
  0.6 17.0 %collective-permute-start.3 = (bf16[256,256]{1,0:T(8,128)(2,1)}, bf16[256,256]{1,0:T(8,128)(2,1)S(1)}, u32[]{:S(2)}, u32[]{:S(2)}) collective-permute-start(bf16[256,256]{1,0:T(8,128)(2,1)} %param.6), channel_id=1, source_target_pairs={{0,3},{1,2},{2,1},{3,0},{4,7},{5,6},{6,5},{7,4},{8,11},{9,10},{10,... | collective-permute-start | bytes 393224 | tf_op jit(solution)/shard_map/ppermute | solution.py:299
  4.3 14.9 %collective-permute-start.1 = (bf16[256,256]{1,0:T(8,128)(2,1)}, bf16[256,256]{1,0:T(8,128)(2,1)S(1)}, u32[]{:S(2)}, u32[]{:S(2)}) collective-permute-start(bf16[256,256]{1,0:T(8,128)(2,1)} %param.6), channel_id=1, source_target_pairs={{0,128},{64,192},{128,0},{192,64},{1,129},{65,193},{129,1},{193,65... | collective-permute-start | bytes 393224 | tf_op jit(solution)/shard_map/ppermute | solution.py:301
  8.5 18.3 %all-to-all-start = ((bf16[8,64,256]{2,1,0:T(8,128)(2,1)}), bf16[8,64,256]{2,1,0:T(8,128)(2,1)S(1)}, u32[]{:S(2)}, u32[]{:S(2)}) async-start(bf16[8,64,256]{2,1,0:T(8,128)(2,1)} %broadcast_in_dim.2), calls=%async_computation | async-start | bytes 524288 | tf_op jit(solution)/shard_map/all_to_all | solution.py:315
  17.6 9.2 %collective-permute-start.5 = (bf16[512,256]{1,0:T(8,128)(2,1)S(1)}, bf16[512,256]{1,0:T(8,128)(2,1)S(1)}, u32[]{:S(2)}, u32[]{:S(2)}) collective-permute-start(bf16[512,256]{1,0:T(8,128)(2,1)S(1)} %constant_dynamic-update-slice_fusion.refs_0_), channel_id=1, source_target_pairs={{0,192},{64,0},{128,64},{192,128},{1,193},{65,1},{129,65},{193,129... | collective-permute-start | bytes 786440 | tf_op jit(solution)/shard_map/ppermute | solution.py:302
  18.6 8.3 %collective-permute-start.4 = (bf16[512,256]{1,0:T(8,128)(2,1)S(1)}, bf16[512,256]{1,0:T(8,128)(2,1)S(1)}, u32[]{:S(2)}, u32[]{:S(2)}) collective-permute-start(bf16[512,256]{1,0:T(8,128)(2,1)S(1)} %constant_dynamic-update-slice_fusion.refs_0_), channel_id=1, source_target_pairs={{0,64},{64,128},{128,192},{192,0},{1,65},{65,129},{129,193},{193,1... | collective-permute-start | bytes 786440 | tf_op jit(solution)/shard_map/ppermute | solution.py:302
  19.2 0.7 copy-start.1
  19.9 6.9 %collective-permute-start.2 = (bf16[288,256]{1,0:T(8,128)(2,1)S(1)}, bf16[288,256]{1,0:T(8,128)(2,1)S(1)}, u32[]{:S(2)}, u32[]{:S(2)}) collective-permute-start(bf16[288,256]{1,0:T(8,128)(2,1)S(1)} %get-tuple-element.13), channel_id=1, source_target_pairs={{0,3},{1,2},{2,1},{3,0},{4,7},{5,6},{6,5},{7,4},{8,11},{9,10},{10,... | collective-permute-start | bytes 442376 | tf_op jit(solution)/shard_map/ppermute | solution.py:314
  26.8 5.2 %collective-permute-start = (bf16[512,256]{1,0:T(8,128)(2,1)S(1)}, bf16[512,256]{1,0:T(8,128)(2,1)S(1)}, u32[]{:S(2)}, u32[]{:S(2)}) collective-permute-start(bf16[512,256]{1,0:T(8,128)(2,1)S(1)} %bitcast.6), channel_id=1, source_target_pairs={{0,1},{1,0},{2,3},{3,2},{4,5},{5,4},{6,7},{7,6},{8,9},{9,8},{10,11... | collective-permute-start | bytes 786440 | tf_op jit(solution)/shard_map/ppermute | solution.py:327
  27.5 6.0 %collective-permute-start.6 = (bf16[2048,256]{1,0:T(8,128)(2,1)S(1)}, bf16[2048,256]{1,0:T(8,128)(2,1)S(1)}, u32[]{:S(2)}, u32[]{:S(2)}) collective-permute-start(bf16[2048,256]{1,0:T(8,128)(2,1)S(1)} %get-tuple-element.14.t_ref.ta_ref), channel_id=1, source_target_pairs={{0,32},{32,0},{1,33},{33,1},{2,34},{34,2},{3,35},{35,3},{4,36},{36... | collective-permute-start | bytes 3145736 | tf_op jit(solution)/shard_map/ppermute | solution.py:326
  33.4 8.9 %copy-start = (f32[2048]{0:T(1024)S(1)}, f32[2048]{0:T(1024)}, u32[]{:S(2)}) copy-start(f32[2048]{0:T(1024)} %param.7) | copy-start | bytes 24580
  36.8 13.4 %all-to-all-start.1 = ((f32[16,8,128]{2,1,0:T(8,128)}), f32[16,8,128]{2,1,0:T(8,128)S(1)}, u32[]{:S(2)}, u32[]{:S(2)}) async-start(f32[16,8,128]{2,1,0:T(8,128)} %get-tuple-element.16), calls=%async_computation.1 | async-start | bytes 131072 | tf_op jit(solution)/shard_map/all_to_all | solution.py:354
  44.8 30.1 %copy-start.2 = (f32[2048]{0:T(1024)S(1)}, f32[2048]{0:T(1024)}, u32[]{:S(2)}) copy-start(f32[2048]{0:T(1024)} %param.8) | copy-start | bytes 24580

commit v5 on v4

--- a/solution.py
+++ b/solution.py
@@ -300,6 +300,7 @@
     mine = jnp.concatenate([target_points, pair_points], axis=0)
     opposite = lax.ppermute(target_points, "x", around(NX, SHIFTS[-1]))
     pieces = [mine] + [lax.ppermute(mine, "x", around(NX, k)) for k in SHIFTS[1:-1]] + [opposite]
+    near_potential = lax.ppermute(potential, "c", around(NC, 1))
     packed, own_potential = pl.pallas_call(
         pack_kernel,
         out_shape=[
@@ -310,7 +311,7 @@
         out_specs=[VMEM] * 2,
         compiler_params=params(16),
         cost_estimate=cost(0.001),
-    )(opposite, potential)
+    )(opposite, near_potential)
     pair_packed = lax.ppermute(packed, "y", across)
     own = lax.all_to_all(copies, "z", 0, 0).reshape(-1, width)
     block = NX * mine.shape[0]

time: 76 us -> 78.4 us (1.032)
  starting transfers between devices: 24.7 us -> 26.5 us
  blocking collectives: 14 us -> 14.9 us
    all_to_all x1, waiting for transfers between devices: 6.74 us -> 4.41 us  [per_device(): own = lax.all_to_all(copies, 'z', 0, 0).reshape(-1, width)]
    ppermute x0 -> x1, starting transfers between devices: none -> 2.08 us  [per_device(): near_potential = lax.ppermute(potential, 'c', around(NC, 1))]
    ppermute x1, waiting for transfers between devices: 0.01 us -> 1.88 us  [per_device(): pair_packed = lax.ppermute(packed, 'y', across)]
    ppermute x1, starting transfers between devices: 2.91 us -> 1.26 us  [per_device(): far = lax.ppermute(near, 'c', around(NC, 1))]
    all_to_all x1, starting transfers between devices: 5.51 us -> 6.98 us  [per_device(): got = lax.all_to_all(sent, ('z', 'y'), 0, 0, axis_index_groups=z_beside)]
    ppermute x0 -> x1, waiting for transfers between devices: none -> 1.04 us  [per_device(): near_potential = lax.ppermute(potential, 'c', around(NC, 1))]
    all_to_all x1, blocking collectives: 14 us -> 14.9 us  [per_device(): lax.all_to_all(sent, ('x', 'c', 'y'), 0, 0, axis_index_groups=xc_across)]
    unnamed x7 -> x5, local copies, waits for them, and re-layouts: 1.62 us -> 0.93 us
  transfers between devices with their start and end apart: 9 -> 10, of which waited for: 3 -> 5; matrix products, arithmetic and copies ran while one was open for 3% -> 3% of each run, Pallas kernels for 8% -> 7%
where the time goes in v5:
time: 78.4 us; the launch traced here: 78 us
  starting transfers between devices  26.5 us (34%)
  Pallas kernels  20.5 us (26%)
  blocking collectives  14.9 us (19%)
  waiting for transfers between devices  12.9 us (16%)
  local copies, waits for them, and re-layouts  2.42 us (3%)
    all_to_all x1, blocking collectives, per_device(): lax.all_to_all(sent, ('x', 'c', 'y'), 0, 0, axis_index_groups=xc_across)  14.9 us
    pallas_call x1, Pallas kernels, per_device(): pl.pallas_call(functools.partial(col_kernel, rate), out_shape=jax.ShapeDt...  10.7 us
    all_to_all x1, starting transfers between devices, per_device(): own = lax.all_to_all(copies, 'z', 0, 0).reshape(-1, width)  8.19 us
    all_to_all x1, starting transfers between devices, per_device(): got = lax.all_to_all(sent, ('z', 'y'), 0, 0, axis_index_groups=z_beside)  6.98 us
    all_to_all x1, waiting for transfers between devices, per_device(): got = lax.all_to_all(sent, ('z', 'y'), 0, 0, axis_index_groups=z_beside)  5.45 us
    all_to_all x1, waiting for transfers between devices, per_device(): own = lax.all_to_all(copies, 'z', 0, 0).reshape(-1, width)  4.41 us
    ppermute x1, starting transfers between devices, per_device(): pair_points = lax.ppermute(target_points, 'y', across)  3.65 us
    pallas_call x1, Pallas kernels, per_device(): pl.pallas_call(functools.partial(row_far, rate), out_shape=[jax.ShapeDtyp...  3.4 us
  transfers between devices with their start and end apart: 10, of which 5 were waited for; matrix products, arithmetic and copies ran while one was open for 3% of the time, Pallas kernels for 7%

profile of v5, /device:TPU:1, one launch (start us, length us, event | category | flops | bytes accessed | tf_op | source)
XLA Modules:
  0.0 78.0 jit_solution(1489348490060975747)
XLA Ops:
  0.6 3.7 %collective-permute-start.4 = (bf16[256,256]{1,0:T(8,128)(2,1)}, bf16[256,256]{1,0:T(8,128)(2,1)S(1)}, u32[]{:S(2)}, u32[]{:S(2)}) collective-permute-start(bf16[256,256]{1,0:T(8,128)(2,1)} %param.6), channel_id=1, source_target_pairs={{0,3},{1,2},{2,1},{3,0},{4,7},{5,6},{6,5},{7,4},{8,11},{9,10},{10,... | collective-permute-start | bytes 393224 | tf_op jit(solution)/shard_map/ppermute | solution.py:299
  4.3 2.7 %collective-permute-start.1 = (bf16[256,256]{1,0:T(8,128)(2,1)}, bf16[256,256]{1,0:T(8,128)(2,1)S(1)}, u32[]{:S(2)}, u32[]{:S(2)}) collective-permute-start(bf16[256,256]{1,0:T(8,128)(2,1)} %param.6), channel_id=1, source_target_pairs={{0,128},{64,192},{128,0},{192,64},{1,129},{65,193},{129,1},{193,65... | collective-permute-start | bytes 393224 | tf_op jit(solution)/shard_map/ppermute | solution.py:301
  7.0 1.5 %broadcast_in_dim.2 = bf16[8,64,256]{2,1,0:T(8,128)(2,1)} broadcast(bf16[64,256]{1,0:T(8,128)(2,1)} %param.5), dimensions={1,2} | broadcast | bytes 294912 | tf_op jit(solution)/shard_map/broadcast_in_dim | solution.py:298
  8.5 8.2 %all-to-all-start = ((bf16[8,64,256]{2,1,0:T(8,128)(2,1)}), bf16[8,64,256]{2,1,0:T(8,128)(2,1)S(1)}, u32[]{:S(2)}, u32[]{:S(2)}) async-start(bf16[8,64,256]{2,1,0:T(8,128)(2,1)} %broadcast_in_dim.2), calls=%async_computation | async-start | bytes 524288 | tf_op jit(solution)/shard_map/all_to_all | solution.py:316
  16.7 0.9 %constant_dynamic-update-slice_fusion.1 = bf16[512,256]{1,0:T(8,128)(2,1)S(1)} fusion(bf16[256,256]{1,0:T(8,128)(2,1)} %param.6), kind=kLoop, calls=%fused_computation.1 | loop fusion | bytes 262144
  17.6 0.0 collective-permute-done.4
  17.6 0.9 %collective-permute-start.6 = (bf16[512,256]{1,0:T(8,128)(2,1)S(1)}, bf16[512,256]{1,0:T(8,128)(2,1)S(1)}, u32[]{:S(2)}, u32[]{:S(2)}) collective-permute-start(bf16[512,256]{1,0:T(8,128)(2,1)S(1)} %constant_dynamic-update-slice_fusion.refs_0_), channel_id=1, source_target_pairs={{0,192},{64,0},{128,64},{192,128},{1,193},{65,1},{129,65},{193,129... | collective-permute-start | bytes 786440 | tf_op jit(solution)/shard_map/ppermute | solution.py:302
  18.6 0.6 collective-permute-start.5
  19.2 2.1 %collective-permute-start.2 = (f32[16,128]{1,0:T(8,128)}, f32[16,128]{1,0:T(8,128)S(1)}, u32[]{:S(2)}, u32[]{:S(2)}) collective-permute-start(f32[16,128]{1,0:T(8,128)} %bitcast.14), channel_id=1, source_target_pairs={{0,32},{32,0},{1,33},{33,1},{2,34},{34,2},{3,35},{35,3},{4,36},{36... | collective-permute-start | bytes 24584 | tf_op jit(solution)/shard_map/ppermute | solution.py:303
  21.3 1.0 %collective-permute-done.2.tp_ref = f32[16,128]{1,0:T(8,128)S(1)} collective-permute-done((f32[16,128]{1,0:T(8,128)}, f32[16,128]{1,0:T(8,128)S(1)}, u32[]{:S(2)}, u32[]{:S(2)}) %collective-permute-start.2) | collective-permute-done | bytes 8224 | tf_op jit(solution)/shard_map/ppermute | solution.py:303
  22.3 0.0 collective-permute-done.1.targets_ref.refs_3_
  22.3 0.1 collective-permute-start.3
  22.4 4.4 %all-to-all-done = bf16[8,64,256]{2,1,0:T(8,128)(2,1)S(1)} async-done(((bf16[8,64,256]{2,1,0:T(8,128)(2,1)}), bf16[8,64,256]{2,1,0:T(8,128)(2,1)S(1)}, u32[]{:S(2)}, u32[]{:S(2)}) %all-to-all-start) | async-done | bytes 262176 | tf_op jit(solution)/shard_map/all_to_all | solution.py:316
  26.8 0.0 collective-permute-start
  26.8 1.9 %collective-permute-done.3.pair_ref = bf16[288,256]{1,0:T(8,128)(2,1)S(1)} collective-permute-done((bf16[288,256]{1,0:T(8,128)(2,1)S(1)}, bf16[288,256]{1,0:T(8,128)(2,1)S(1)}, u32[]{:S(2)}, u32[]{:S(2)}) %collective-permute-start.3) | collective-permute-done | bytes 147488 | tf_op jit(solution)/shard_map/ppermute | solution.py:315
  28.7 0.0 collective-permute-done.6.refs_2_
  28.7 0.0 collective-permute-done.5.refs_1_
  28.7 0.6 shard_map.69
  29.3 1.3 %collective-permute-start.7 = (bf16[2048,256]{1,0:T(8,128)(2,1)S(1)}, bf16[2048,256]{1,0:T(8,128)(2,1)S(1)}, u32[]{:S(2)}, u32[]{:S(2)}) collective-permute-start(bf16[2048,256]{1,0:T(8,128)(2,1)S(1)} %get-tuple-element.14.t_ref.ta_ref), channel_id=1, source_target_pairs={{0,32},{32,0},{1,33},{33,1},{2,34},{34,2},{3,35},{35,3},{4,36},{36... | collective-permute-start | bytes 3145736 | tf_op jit(solution)/shard_map/ppermute | solution.py:327
  30.6 1.4 %shard_map.70.own_near = f32[4,128]{1,0:T(4,128)S(1)} custom-call(bf16[512,256]{1,0:T(8,128)(2,1)S(1)} %bitcast.8, bf16[2048,256]{1,0:T(8,128)(2,1)S(1)} %get-tuple-element.14.t_ref.ta_ref, f32[4096,128]{1,0:T(8,128)S(1)} %get-tuple-element.15.bias_ref), custom_call_target="tpu_custom_call" | custom-call | flops 30000001024 | bytes 1048576 | tf_op jit(solution)/shard_map/pallas_call | solution.py:335
  32.0 0.1 collective-permute-done.s_ref.pair_ref.s1
  32.0 1.4 %shard_map.71.pair_near = f32[4,128]{1,0:T(4,128)S(1)} custom-call(bf16[512,256]{1,0:T(8,128)(2,1)S(1)} %collective-permute-done.s_ref.pair_ref.s1, bf16[2048,256]{1,0:T(8,128)(2,1)S(1)} %get-tuple-element.14.t_ref.ta_ref, f32[4096,128]{1,0:T(8,128)S(1)} %get-tuple-element.15.bias_ref), custom_call_target="tpu_custom_call" | custom-call | bytes 262144 | tf_op jit(solution)/shard_map/pallas_call | solution.py:335
  33.4 0.0 copy-start
  33.4 0.0 collective-permute-done.7.t_ref.tb_ref
  33.4 3.4 %shard_map.72 = (f32[16,8,128]{2,1,0:T(8,128)}, f32[8,128]{1,0:T(8,128)S(1)}) custom-call(bf16[512,256]{1,0:T(8,128)(2,1)S(1)} %bitcast.9, bf16[512,256]{1,0:T(8,128)(2,1)S(1)} %collective-permute-done.s_ref.pair_ref.s1, bf16[2048,256]{1,0:T(8,128)(2,1)S(1)} %collective-permute-done.7.t_ref.tb_ref, f32[4096,128]{1,0:T(8,128)S(1)} %get-tuple-element.15.bias_ref, ...), custom_call_target="tpu_custom_call" | custom-call | bytes 16777216 | tf_op jit(solution)/shard_map/pallas_call | solution.py:346
  36.8 7.0 %all-to-all-start.1 = ((f32[16,8,128]{2,1,0:T(8,128)}), f32[16,8,128]{2,1,0:T(8,128)S(1)}, u32[]{:S(2)}, u32[]{:S(2)}) async-start(f32[16,8,128]{2,1,0:T(8,128)} %get-tuple-element.16), calls=%async_computation.1 | async-start | bytes 131072 | tf_op jit(solution)/shard_map/all_to_all | solution.py:355
  43.8 2.4 %shard_map.73 = (f32[32,128]{1,0:T(8,128)S(1)}, f32[8,128]{1,0:T(8,128)S(1)}) custom-call(f32[8,128]{1,0:T(8,128)S(1)} %get-tuple-element.17.rows_ref, f32[16,128]{1,0:T(8,128)S(1)} %bitcast.12, bf16[512,256]{1,0:T(8,128)(2,1)S(1)} %bitcast.10, bf16[512,256]{1,0:T(8,128)(2,1)S(1)} %collective-permute-done.s_ref.pair_ref.s1, ...), custom_call_target="tpu_custom_call" | custom-call | bytes 16777216 | tf_op jit(solution)/shard_map/pallas_call | solution.py:359
  46.2 0.0 copy-start.1
  46.3 5.5 %all-to-all-done.1.got_ref = f32[16,8,128]{2,1,0:T(8,128)S(1)} async-done(((f32[16,8,128]{2,1,0:T(8,128)}), f32[16,8,128]{2,1,0:T(8,128)S(1)}, u32[]{:S(2)}, u32[]{:S(2)}) %all-to-all-start.1) | async-done | bytes 65568 | tf_op jit(solution)/shard_map/all_to_all | solution.py:355
  51.7 10.7 %shard_map.74 = f32[16,24,128]{2,1,0:T(8,128)S(1)} custom-call(f32[16,8,128]{2,1,0:T(8,128)S(1)} %all-to-all-done.1.got_ref, f32[8,128]{1,0:T(8,128)S(1)} %get-tuple-element.17.rows_ref, f32[8,128]{1,0:T(8,128)S(1)} %get-tuple-element.18.ready_ref, f32[32,128]{1,0:T(8,128)S(1)} %get-tuple-element.19.top_ref, bf16[512,256]{1,0:T(8,128)(2,1)S(1)} %bitcast.11, ...), custom_call_target="tpu_custom_call" | custom-call | bytes 16777216 | tf_op jit(solution)/shard_map/pallas_call | solution.py:368
  62.4 14.9 %all_to_all.15.got_ref = f32[16,24,128]{2,1,0:T(8,128)S(1)} all-to-all(f32[16,24,128]{2,1,0:T(8,128)S(1)} %shard_map.74), channel_id=1, replica_groups={{0,3,32,35,64,67,96,99,128,131,160,163,192,195,224,227},{1,2,33,34,65,6..., dimensions={0} | all-to-all | bytes 393216 | tf_op jit(solution)/shard_map/all_to_all | solution.py:377
  77.3 0.7 shard_map.75
  (4 shorter events, 0.0 us)
Async XLA Ops:
  0.6 17.0 %collective-permute-start.4 = (bf16[256,256]{1,0:T(8,128)(2,1)}, bf16[256,256]{1,0:T(8,128)(2,1)S(1)}, u32[]{:S(2)}, u32[]{:S(2)}) collective-permute-start(bf16[256,256]{1,0:T(8,128)(2,1)} %param.6), channel_id=1, source_target_pairs={{0,3},{1,2},{2,1},{3,0},{4,7},{5,6},{6,5},{7,4},{8,11},{9,10},{10,... | collective-permute-start | bytes 393224 | tf_op jit(solution)/shard_map/ppermute | solution.py:299
  4.3 18.0 %collective-permute-start.1 = (bf16[256,256]{1,0:T(8,128)(2,1)}, bf16[256,256]{1,0:T(8,128)(2,1)S(1)}, u32[]{:S(2)}, u32[]{:S(2)}) collective-permute-start(bf16[256,256]{1,0:T(8,128)(2,1)} %param.6), channel_id=1, source_target_pairs={{0,128},{64,192},{128,0},{192,64},{1,129},{65,193},{129,1},{193,65... | collective-permute-start | bytes 393224 | tf_op jit(solution)/shard_map/ppermute | solution.py:301
  8.5 18.3 %all-to-all-start = ((bf16[8,64,256]{2,1,0:T(8,128)(2,1)}), bf16[8,64,256]{2,1,0:T(8,128)(2,1)S(1)}, u32[]{:S(2)}, u32[]{:S(2)}) async-start(bf16[8,64,256]{2,1,0:T(8,128)(2,1)} %broadcast_in_dim.2), calls=%async_computation | async-start | bytes 524288 | tf_op jit(solution)/shard_map/all_to_all | solution.py:316
  17.6 11.1 %collective-permute-start.6 = (bf16[512,256]{1,0:T(8,128)(2,1)S(1)}, bf16[512,256]{1,0:T(8,128)(2,1)S(1)}, u32[]{:S(2)}, u32[]{:S(2)}) collective-permute-start(bf16[512,256]{1,0:T(8,128)(2,1)S(1)} %constant_dynamic-update-slice_fusion.refs_0_), channel_id=1, source_target_pairs={{0,192},{64,0},{128,64},{192,128},{1,193},{65,1},{129,65},{193,129... | collective-permute-start | bytes 786440 | tf_op jit(solution)/shard_map/ppermute | solution.py:302
  18.6 10.1 %collective-permute-start.5 = (bf16[512,256]{1,0:T(8,128)(2,1)S(1)}, bf16[512,256]{1,0:T(8,128)(2,1)S(1)}, u32[]{:S(2)}, u32[]{:S(2)}) collective-permute-start(bf16[512,256]{1,0:T(8,128)(2,1)S(1)} %constant_dynamic-update-slice_fusion.refs_0_), channel_id=1, source_target_pairs={{0,64},{64,128},{128,192},{192,0},{1,65},{65,129},{129,193},{193,1... | collective-permute-start | bytes 786440 | tf_op jit(solution)/shard_map/ppermute | solution.py:302
  19.2 3.1 %collective-permute-start.2 = (f32[16,128]{1,0:T(8,128)}, f32[16,128]{1,0:T(8,128)S(1)}, u32[]{:S(2)}, u32[]{:S(2)}) collective-permute-start(f32[16,128]{1,0:T(8,128)} %bitcast.14), channel_id=1, source_target_pairs={{0,32},{32,0},{1,33},{33,1},{2,34},{34,2},{3,35},{35,3},{4,36},{36... | collective-permute-start | bytes 24584 | tf_op jit(solution)/shard_map/ppermute | solution.py:303
  22.3 6.4 %collective-permute-start.3 = (bf16[288,256]{1,0:T(8,128)(2,1)S(1)}, bf16[288,256]{1,0:T(8,128)(2,1)S(1)}, u32[]{:S(2)}, u32[]{:S(2)}) collective-permute-start(bf16[288,256]{1,0:T(8,128)(2,1)S(1)} %get-tuple-element.13), channel_id=1, source_target_pairs={{0,3},{1,2},{2,1},{3,0},{4,7},{5,6},{6,5},{7,4},{8,11},{9,10},{10,... | collective-permute-start | bytes 442376 | tf_op jit(solution)/shard_map/ppermute | solution.py:315
  26.8 5.2 %collective-permute-start = (bf16[512,256]{1,0:T(8,128)(2,1)S(1)}, bf16[512,256]{1,0:T(8,128)(2,1)S(1)}, u32[]{:S(2)}, u32[]{:S(2)}) collective-permute-start(bf16[512,256]{1,0:T(8,128)(2,1)S(1)} %bitcast.6), channel_id=1, source_target_pairs={{0,1},{1,0},{2,3},{3,2},{4,5},{5,4},{6,7},{7,6},{8,9},{9,8},{10,11... | collective-permute-start | bytes 786440 | tf_op jit(solution)/shard_map/ppermute | solution.py:328
  29.3 4.1 %collective-permute-start.7 = (bf16[2048,256]{1,0:T(8,128)(2,1)S(1)}, bf16[2048,256]{1,0:T(8,128)(2,1)S(1)}, u32[]{:S(2)}, u32[]{:S(2)}) collective-permute-start(bf16[2048,256]{1,0:T(8,128)(2,1)S(1)} %get-tuple-element.14.t_ref.ta_ref), channel_id=1, source_target_pairs={{0,32},{32,0},{1,33},{33,1},{2,34},{34,2},{3,35},{35,3},{4,36},{36... | collective-permute-start | bytes 3145736 | tf_op jit(solution)/shard_map/ppermute | solution.py:327
  33.4 10.4 %copy-start = (f32[2048]{0:T(1024)S(1)}, f32[2048]{0:T(1024)}, u32[]{:S(2)}) copy-start(f32[2048]{0:T(1024)} %param.7) | copy-start | bytes 24580
  36.8 14.9 %all-to-all-start.1 = ((f32[16,8,128]{2,1,0:T(8,128)}), f32[16,8,128]{2,1,0:T(8,128)S(1)}, u32[]{:S(2)}, u32[]{:S(2)}) async-start(f32[16,8,128]{2,1,0:T(8,128)} %get-tuple-element.16), calls=%async_computation.1 | async-start | bytes 131072 | tf_op jit(solution)/shard_map/all_to_all | solution.py:355
  46.2 31.0 %copy-start.1 = (f32[2048]{0:T(1024)S(1)}, f32[2048]{0:T(1024)}, u32[]{:S(2)}) copy-start(f32[2048]{0:T(1024)} %param.8) | copy-start | bytes 24580
